TPU v7x, 128 devices: a whole 4x4x4 slice. The times are simulated.
128 devices in a mesh: dp: 16 (over y, x), seq: 8 (over z, core).
Axes of the slice: x: 4, y: 4, z: 4, core: 2. Of those that a mesh axis runs over, the one named last changes fastest.
Arguments:
- activations: bfloat16 [16, 1024, 1536], P('dp', 'seq'), may hold values from -6 to 6
- convolution_weight: bfloat16 [5, 1536, 384], replicated, may hold values from -0.0625 to 0.0625
- out_weight: bfloat16 [384, 1536], replicated, may hold values from -0.3125 to 0.3125
- cotangent: bfloat16 [16, 1024, 1536], P('dp', 'seq'), may hold values from -6 to 6
- donor_pos: int32 [16, 448], P('dp'), may hold values from 0 to 1023, as said below
- acceptor_pos: int32 [16, 448], P('dp'), may hold values from 0 to 1023, as said below
- junction_flags: int32 [16, 448], P('dp'), may hold values 0 or 1
- junction_grad: float32 [16, 448], P('dp'), may hold values from -72 to 72
Outputs:
- block_out: bfloat16 [16, 1024, 1536], P('dp', 'seq')
- input_grad: bfloat16 [16, 1024, 1536], P('dp', 'seq')
- conv_grad: float32 [5, 1536, 384], P(None, ('dp', 'seq'))
- out_grad: float32 [384, 1536], P(('dp', 'seq'))
Inputs may be any that keep to these rules, and one draw needn't show every extreme that they name: `donor_pos`: of each sequence's entries, exactly 56 have their donor among the 128 positions of each device. For two devices along seq, at most 16 entries have their donor on the first and their acceptor on the second, and for every first device exactly 16 for some second device. Padding entries carry positions too. `acceptor_pos`: the acceptor of an entry may lie before or after its donor, on any device.
All inputs are finite; a program needn't handle non-finite values. No bound on the sum of `junction_flags` on one device may be relied on, other than what follows from the above.
Results may differ from a plain program's by a relative error of at most 0.013.
Values may be sent and summed in bfloat16 or wider, within the bound.
A program may use at most 128 MiB of HBM per device.

v0:
```python
import jax
import jax.numpy as jnp
from jax import lax
from jax.sharding import PartitionSpec as P

KERNEL_WIDTH = 5
DILATION_STEP = 32
CAP = 16


EPS = 1e-06
SLOPE = 0.7978845608028654
CUBIC = 0.044715


def padded(shard, sides, width):
    for axis, dim in sides:
        peers, length = (lax.axis_size(axis), shard.shape[dim])
        up = [(i, (i + 1) % peers) for i in range(peers - 1)]
        down = [(j, i) for i, j in up]
        last = lax.slice_in_dim(shard, length - width, length, axis=dim)
        first = lax.slice_in_dim(shard, 0, width, axis=dim)
        before = lax.ppermute(last, axis, up)
        after = lax.ppermute(first, axis, down)
        shard = jnp.concatenate([before, shard, after], axis=dim)
    return shard


def gelu_tanh(values):
    return 0.5 * values * (1.0 + jnp.tanh(SLOPE * (values + CUBIC * values * values * values)))


def gelu_slope(values):
    curved = jnp.tanh(SLOPE * (values + CUBIC * values * values * values))
    return 0.5 * (1.0 + curved) + 0.5 * values * (1.0 - curved * curved) * SLOPE * (
        1.0 + 3.0 * CUBIC * values * values
    )


def junction_slots(donors, accepts, flag_row, grad_row, device, resident_rows, seq_count, channels):
    donor_owner = donors // resident_rows
    accept_owner = accepts // resident_rows
    pairing = donor_owner * seq_count + accept_owner
    entries = jnp.arange(donors.shape[0])
    ranking = jnp.sum(
        (pairing[:, None] == pairing[None, :]) & (entries[None, :] < entries[:, None]), axis=1
    )
    scaled = grad_row * flag_row.astype(jnp.float32) * channels ** (-0.5)
    slot_ids = jnp.arange(seq_count * CAP)
    donor_hit = (donor_owner == device)[:, None] & (
        (accept_owner * CAP + ranking)[:, None] == slot_ids[None, :]
    )
    accept_hit = (accept_owner == device)[:, None] & (
        (donor_owner * CAP + ranking)[:, None] == slot_ids[None, :]
    )
    donor_rows = jnp.sum(
        jnp.where(donor_hit, (donors - device * resident_rows)[:, None], 0), axis=0
    )
    accept_rows = jnp.sum(
        jnp.where(accept_hit, (accepts - device * resident_rows)[:, None], 0), axis=0
    )
    donor_coef = jnp.sum(jnp.where(donor_hit, scaled[:, None], 0.0), axis=0)
    accept_coef = jnp.sum(jnp.where(accept_hit, scaled[:, None], 0.0), axis=0)
    return (
        donor_rows,
        jnp.any(donor_hit, axis=0),
        donor_coef,
        accept_rows,
        jnp.any(accept_hit, axis=0),
        accept_coef,
    )


def pick_rows(sequence_rows, row_index, valid_slot):
    return jnp.where(
        valid_slot[:, None],
        jnp.take(sequence_rows, row_index, axis=0),
        jnp.zeros((), sequence_rows.dtype),
    )


def place_rows(row_index, valid_slot, slot_weight, resident_rows):
    matching = (row_index[None, :] == jnp.arange(resident_rows)[:, None]) & valid_slot[None, :]
    return jnp.where(matching, slot_weight[None, :], 0.0)


def shards(
    activations,
    convolution_weight,
    out_weight,
    cotangent,
    donor_pos,
    acceptor_pos,
    junction_flags,
    junction_grad,
):
    seq_batch = activations.shape[0]
    resident_rows = activations.shape[1]
    channels = activations.shape[2]
    inner = out_weight.shape[0]
    seq_count = lax.axis_size("seq")
    device = lax.axis_index("seq")
    border_width = KERNEL_WIDTH // 2 * DILATION_STEP
    act_float = activations.astype(jnp.float32)
    inverse = lax.rsqrt(jnp.mean(act_float * act_float, axis=-1, keepdims=True) + EPS)
    normed = (act_float * inverse).astype(jnp.bfloat16)
    padded_input = padded(normed, (("seq", 1),), border_width)
    preactivation = jnp.zeros((seq_batch, resident_rows, inner), jnp.float32)
    for kernel_tap_index in range(KERNEL_WIDTH):
        sliding_window = padded_input[
            :, kernel_tap_index * DILATION_STEP : kernel_tap_index * DILATION_STEP + resident_rows
        ]
        preactivation = preactivation + jnp.einsum(
            "bpc,cm->bpm",
            sliding_window,
            convolution_weight[kernel_tap_index],
            preferred_element_type=jnp.float32,
        )
    hidden = gelu_tanh(preactivation).astype(jnp.bfloat16)
    block_out = (
        act_float
        + jnp.einsum("bpm,mc->bpc", hidden, out_weight, preferred_element_type=jnp.float32)
    ).astype(jnp.bfloat16)
    slot_fn = jax.vmap(junction_slots, in_axes=(0, 0, 0, 0, None, None, None, None))
    donor_rows, donor_valid, donor_coef, accept_rows, accept_valid, accept_coef = slot_fn(
        donor_pos,
        acceptor_pos,
        junction_flags,
        junction_grad,
        device,
        resident_rows,
        seq_count,
        channels,
    )
    sent_donor = jax.vmap(pick_rows)(block_out, donor_rows, donor_valid)
    sent_accept = jax.vmap(pick_rows)(block_out, accept_rows, accept_valid)
    place_fn = jax.vmap(place_rows, in_axes=(0, 0, 0, None))
    donor_place = place_fn(donor_rows, donor_valid, donor_coef, resident_rows)
    slot_total = seq_count * CAP
    outgoing = jnp.stack(
        (
            sent_donor.reshape(seq_batch, seq_count, CAP, channels),
            sent_accept.reshape(seq_batch, seq_count, CAP, channels),
        ),
        axis=2,
    )
    arrived = lax.all_to_all(outgoing, "seq", split_axis=1, concat_axis=1, tiled=True)
    far_accept = arrived[:, :, 1].reshape(seq_batch, slot_total, channels).astype(jnp.float32)
    far_donor = arrived[:, :, 0].reshape(seq_batch, slot_total, channels).astype(jnp.float32)
    accept_place = place_fn(accept_rows, accept_valid, accept_coef, resident_rows)
    pulled = jnp.einsum("bps,bsc->bpc", donor_place, far_accept, precision=lax.Precision.HIGHEST)
    pulled = pulled + jnp.einsum(
        "bps,bsc->bpc", accept_place, far_donor, precision=lax.Precision.HIGHEST
    )
    upstream = (cotangent.astype(jnp.float32) + pulled).astype(jnp.bfloat16)
    grad_hidden = jnp.einsum(
        "bpc,mc->bpm", upstream, out_weight, preferred_element_type=jnp.float32
    )
    preactivation_gradient = (grad_hidden * gelu_slope(preactivation)).astype(jnp.bfloat16)
    out_grad = jnp.einsum("bpm,bpc->mc", hidden, upstream, preferred_element_type=jnp.float32)
    grad_pad = padded(preactivation_gradient, (("seq", 1),), border_width)
    grad_normed = jnp.zeros((seq_batch, resident_rows, channels), jnp.float32)
    convolution_terms = []
    for kernel_tap_index in range(KERNEL_WIDTH):
        offset_start = (KERNEL_WIDTH - 1 - kernel_tap_index) * DILATION_STEP
        grad_normed = grad_normed + jnp.einsum(
            "bpm,cm->bpc",
            grad_pad[:, offset_start : offset_start + resident_rows],
            convolution_weight[kernel_tap_index],
            preferred_element_type=jnp.float32,
        )
        sliding_window = padded_input[
            :, kernel_tap_index * DILATION_STEP : kernel_tap_index * DILATION_STEP + resident_rows
        ]
        convolution_terms.append(
            jnp.einsum(
                "bpc,bpm->cm",
                sliding_window,
                preactivation_gradient,
                preferred_element_type=jnp.float32,
            )
        )
    conv_grad = jnp.stack(convolution_terms)
    spread = jnp.mean(grad_normed * act_float, axis=-1, keepdims=True)
    input_grad = (
        upstream.astype(jnp.float32)
        + inverse * grad_normed
        - inverse * inverse * inverse * act_float * spread
    ).astype(jnp.bfloat16)
    conv_shard, out_shard = (
        lax.psum_scatter(conv_grad, ("dp", "seq"), scatter_dimension=1, tiled=True),
        lax.psum_scatter(out_grad, ("dp", "seq"), scatter_dimension=0, tiled=True),
    )
    return (block_out, input_grad, conv_shard, out_shard)


def solution(mesh):
    in_specs = (
        P("dp", "seq", None),
        P(),
        P(),
        P("dp", "seq", None),
        P("dp", None),
        P("dp", None),
        P("dp", None),
        P("dp", None),
    )
    out_specs = (
        P("dp", "seq", None),
        P("dp", "seq", None),
        P(None, ("dp", "seq"), None),
        P(("dp", "seq"), None),
    )
    return jax.shard_map(shards, mesh=mesh, in_specs=in_specs, out_specs=out_specs, check_vma=False)
```

profile of v0, /device:TPU:0, one launch (start us, length us, event | category | flops | bytes accessed | tf_op | source)
XLA Modules:
  0.0 252.3 jit_solution(13624487994840748314)
XLA Ops:
  7.2 1.3 fusion.50
  8.4 0.5 multiply_multiply_fusion.2
  9.0 1.1 fusion.51
  10.1 1.3 collective-permute-start.1
  11.4 3.0 %collective-permute-start = (bf16[1,64,1536]{2,1,0:T(8,128)(2,1)S(1)}, bf16[1,64,1536]{2,1,0:T(8,128)(2,1)S(1)}, u32[]{:S(2)}, u32[]{:S(2)}) collective-permute-start(bf16[1,64,1536]{2,1,0:T(8,128)(2,1)S(1)} %get-tuple-element.15), channel_id=1, source_target_pairs={{0,1},{1,2},{2,3},{3,4},{4,5},{5,6},{6,7},{8,9},{9,10},{10,11},{11... | collective-permute-start | bytes 589832 | tf_op jit(solution)/shard_map/ppermute | solution.py:23
  14.5 0.7 compare_reduce_fusion
  15.3 0.7 broadcast_subtract_fusion
  16.2 0.3 select_reduce_fusion.1
  16.5 0.5 and_bitcast_fusion
  17.0 0.8 fusion.72
  17.8 1.7 fusion.17
  19.5 0.7 fusion.70
  20.6 0.6 and_bitcast_fusion.1
  21.2 1.6 fusion.11
  22.8 1.6 fusion.14
  24.5 1.6 fusion.21
  26.1 1.7 fusion.35
  27.8 0.7 copy-done.3
  28.5 0.4 fusion.9
  28.9 1.9 gather_fusion.1
  30.8 1.9 gather_fusion
  32.7 0.8 fusion.65
  33.5 0.8 fusion.66
  34.4 1.0 pad_maximum_fusion
  35.3 6.1 %all-to-all-start = ((bf16[1,8,2,16,1536]{4,3,2,0,1:T(8,128)(2,1)}), bf16[1,8,2,16,1536]{4,3,2,0,1:T(8,128)(2,1)S(1)}, u32[]{:S(2)}, u32[]{:S(2)}) async-start(bf16[1,8,2,16,1536]{4,3,2,0,1:T(8,128)(2,1)} %pad_maximum_fusion), calls=%async_computation | async-start | bytes 1572864 | tf_op jit(solution)/shard_map/all_to_all | solution.py:147
  41.4 0.7 multiply_multiply_fusion.1
  42.1 1.6 select_reduce_fusion
  43.7 10.9 %all-to-all-done = bf16[1,8,2,16,1536]{4,3,2,0,1:T(8,128)(2,1)S(1)} async-done(((bf16[1,8,2,16,1536]{4,3,2,0,1:T(8,128)(2,1)}), bf16[1,8,2,16,1536]{4,3,2,0,1:T(8,128)(2,1)S(1)}, u32[]{:S(2)}, u32[]{:S(2)}) %all-to-all-start) | async-done | bytes 786464 | tf_op jit(solution)/shard_map/all_to_all | solution.py:147
  54.6 1.2 fusion.95
  55.8 1.5 fusion.8
  57.3 1.4 fusion.38
  58.8 2.0 fusion.62
  60.8 2.0 fusion.4
  62.8 1.9 fusion.3
  64.6 1.9 fusion.2
  66.6 1.9 fusion.1
  68.5 1.9 fusion
  70.4 1.3 collective-permute-start.2
  71.8 3.0 %collective-permute-start.3 = (bf16[1,64,384]{2,1,0:T(8,128)(2,1)S(1)}, bf16[1,64,384]{2,1,0:T(8,128)(2,1)S(1)}, u32[]{:S(2)}, u32[]{:S(2)}) collective-permute-start(bf16[1,64,384]{2,1,0:T(8,128)(2,1)S(1)} %get-tuple-element.17), channel_id=1, source_target_pairs={{0,1},{1,2},{2,3},{3,4},{4,5},{5,6},{6,7},{8,9},{9,10},{10,11},{11... | collective-permute-start | bytes 147464 | tf_op jit(solution)/shard_map/ppermute | solution.py:23
  74.8 1.8 fusion.19
  76.6 1.8 convolution_add_fusion.3
  78.4 1.9 convolution_add_fusion.2
  80.3 1.8 convolution_add_fusion.1
  82.1 1.9 fusion.55
  84.0 1.1 fusion.54
  85.1 157.3 %all-reduce.5.cloned.1.call-done = (f32[5,1536,384]{2,1,0:T(8,128)}, f32[384,1536]{1,0:T(8,128)}) async-done(((f32[5,1536,384]{2,1,0:T(8,128)}, f32[384,1536]{1,0:T(8,128)}), (f32[5,1536,384]{2,1,0:T(8,128)}, f32[384,1536]{1,0:T(8,128)})) %all-reduce.5.cloned.1.call-update) | async-done | bytes 14155792
  242.4 1.6 constant_dynamic-slice_fusion.1
  244.0 1.5 constant_dynamic-slice_fusion
  (45 shorter events, 0.8 us)
Async XLA Ops:
  7.2 21.3 %copy-start = (bf16[384,1536]{1,0:T(8,128)(2,1)S(1)}, bf16[384,1536]{1,0:T(8,128)(2,1)}, u32[]{:S(2)}) copy-start(bf16[384,1536]{1,0:T(8,128)(2,1)} %param.12) | copy-start | bytes 3538948
  9.0 5.5 %copy-start.10 = (f32[128]{0:T(128)}, f32[128]{0:T(128)S(1)}, u32[]{:S(2)}) copy-start(f32[128]{0:T(128)S(1)} %get-tuple-element.22) | copy-start | bytes 1540
  10.1 11.0 %collective-permute-start.1 = (bf16[1,64,1536]{2,1,0:T(8,128)(2,1)S(1)}, bf16[1,64,1536]{2,1,0:T(8,128)(2,1)S(1)}, u32[]{:S(2)}, u32[]{:S(2)}) collective-permute-start(bf16[1,64,1536]{2,1,0:T(8,128)(2,1)S(1)} %get-tuple-element.16), channel_id=1, source_target_pairs={{1,0},{2,1},{3,2},{4,3},{5,4},{6,5},{7,6},{9,8},{10,9},{11,10},{12... | collective-permute-start | bytes 589832 | tf_op jit(solution)/shard_map/ppermute | solution.py:24
  11.4 13.0 %collective-permute-start = (bf16[1,64,1536]{2,1,0:T(8,128)(2,1)S(1)}, bf16[1,64,1536]{2,1,0:T(8,128)(2,1)S(1)}, u32[]{:S(2)}, u32[]{:S(2)}) collective-permute-start(bf16[1,64,1536]{2,1,0:T(8,128)(2,1)S(1)} %get-tuple-element.15), channel_id=1, source_target_pairs={{0,1},{1,2},{2,3},{3,4},{4,5},{5,6},{6,7},{8,9},{9,10},{10,11},{11... | collective-permute-start | bytes 589832 | tf_op jit(solution)/shard_map/ppermute | solution.py:23
  15.2 12.6 %copy-start.5 = (pred[448]{0:T(512)(128)(4,1)}, pred[448]{0:T(512)(128)(4,1)S(1)}, u32[]{:S(2)}) copy-start(pred[448]{0:T(512)(128)(4,1)S(1)} %get-tuple-element.11) | copy-start | bytes 1348
  15.2 12.6 %copy-start.7 = (pred[448]{0:T(512)(128)(4,1)}, pred[448]{0:T(512)(128)(4,1)S(1)}, u32[]{:S(2)}) copy-start(pred[448]{0:T(512)(128)(4,1)S(1)} %get-tuple-element.25) | copy-start | bytes 1348
  16.5 3.0 %copy-start.9 = (s32[128]{0:T(128)}, s32[128]{0:T(128)S(1)}, u32[]{:S(2)}) copy-start(s32[128]{0:T(128)S(1)} %select_reduce_fusion.1) | copy-start | bytes 1540
  17.8 10.7 %copy-start.2 = (bf16[1,128,1536]{2,1,0:T(8,128)(2,1)S(1)}, bf16[1,128,1536]{2,1,0:T(8,128)(2,1)}, u32[]{:S(2)}) copy-start(bf16[1,128,1536]{2,1,0:T(8,128)(2,1)} %param.10) | copy-start | bytes 1179652
  20.5 8.4 %copy-start.8 = (s32[128]{0:T(128)}, s32[128]{0:T(128)S(1)}, u32[]{:S(2)}) copy-start(s32[128]{0:T(128)S(1)} %select_reduce_fusion.3) | copy-start | bytes 1540
  27.8 0.7 copy-start.3
  28.9 6.4 %copy-start.1 = (bf16[1,128,1536]{2,1,0:T(8,128)(2,1)}, bf16[1,128,1536]{2,1,0:T(8,128)(2,1)S(1)}, u32[]{:S(2)}) copy-start(bf16[1,128,1536]{2,1,0:T(8,128)(2,1)S(1)} %fusion.9) | copy-start | bytes 1179652
  30.8 11.3 %copy-start.6 = (pred[448]{0:T(512)(128)(4,1)S(1)}, pred[448]{0:T(512)(128)(4,1)}, u32[]{:S(2)}) copy-start(pred[448]{0:T(512)(128)(4,1)} %copy-done.5) | copy-start | bytes 1348
  35.3 19.2 %all-to-all-start = ((bf16[1,8,2,16,1536]{4,3,2,0,1:T(8,128)(2,1)}), bf16[1,8,2,16,1536]{4,3,2,0,1:T(8,128)(2,1)S(1)}, u32[]{:S(2)}, u32[]{:S(2)}) async-start(bf16[1,8,2,16,1536]{4,3,2,0,1:T(8,128)(2,1)} %pad_maximum_fusion), calls=%async_computation | async-start | bytes 1572864 | tf_op jit(solution)/shard_map/all_to_all | solution.py:147
  41.4 201.0 %all-reduce.5.cloned.1.call-start = ((), (), s32[]{:S(2)}) async-start(), calls=%async_computation.1 | async-start | bytes 28311552
  54.5 4.2 %copy-start.4 = (f32[128,384]{1,0:T(8,128)S(1)}, f32[128,384]{1,0:T(8,128)}, u32[]{:S(2)}) copy-start(f32[128,384]{1,0:T(8,128)} %copy-done.3) | copy-start | bytes 589828
  70.4 4.3 %collective-permute-start.2 = (bf16[1,64,384]{2,1,0:T(8,128)(2,1)S(1)}, bf16[1,64,384]{2,1,0:T(8,128)(2,1)S(1)}, u32[]{:S(2)}, u32[]{:S(2)}) collective-permute-start(bf16[1,64,384]{2,1,0:T(8,128)(2,1)S(1)} %get-tuple-element.18), channel_id=1, source_target_pairs={{1,0},{2,1},{3,2},{4,3},{5,4},{6,5},{7,6},{9,8},{10,9},{11,10},{12... | collective-permute-start | bytes 147464 | tf_op jit(solution)/shard_map/ppermute | solution.py:24
  71.8 8.6 %collective-permute-start.3 = (bf16[1,64,384]{2,1,0:T(8,128)(2,1)S(1)}, bf16[1,64,384]{2,1,0:T(8,128)(2,1)S(1)}, u32[]{:S(2)}, u32[]{:S(2)}) collective-permute-start(bf16[1,64,384]{2,1,0:T(8,128)(2,1)S(1)} %get-tuple-element.17), channel_id=1, source_target_pairs={{0,1},{1,2},{2,3},{3,4},{4,5},{5,6},{6,7},{8,9},{9,10},{10,11},{11... | collective-permute-start | bytes 147464 | tf_op jit(solution)/shard_map/ppermute | solution.py:23
  76.6 7.4 %copy-start.11 = (f32[128]{0:T(128)S(1)}, f32[128]{0:T(128)}, u32[]{:S(2)}) copy-start(f32[128]{0:T(128)} %copy-done.10) | copy-start | bytes 1540
  76.6 7.4 %copy-start.12 = (f32[128]{0:T(128)S(1)}, f32[128]{0:T(128)}, u32[]{:S(2)}) copy-start(f32[128]{0:T(128)} %get-tuple-element.21) | copy-start | bytes 1540
Sparse Core Ops, SparseCore 0:
  70.5 171.8 all-reduce.4
where the time goes:
time: 254 us; the launch traced here: 252 us
  waiting for transfers between devices  168 us (66%)
  matrix products  33.5 us (13%)
  starting transfers between devices  14.8 us (6%)
  between operations  14.4 us (6%)
  other arithmetic  13.7 us (5%)
  local copies, waits for them, and re-layouts  7.72 us (3%)
    unnamed x2, waiting for transfers between devices  157 us
    all_to_all x1, waiting for transfers between devices, shards(): lax.all_to_all(outgoing, 'seq', split_axis=1, concat_axis=1, tiled=True)  10.9 us
    dot_general x5, matrix products, shards(): jnp.einsum('bpc,bpm->cm', sliding_window, preactivation_gradient, preferr...  9.65 us
    dot_general x5, matrix products, shards(): jnp.einsum('bpm,cm->bpc', grad_pad[:, offset_start:offset_start + residen...  9.12 us
    dot_general x5, matrix products, shards(): jnp.einsum('bpc,cm->bpm', sliding_window, convolution_weight[kernel_tap_i...  8.27 us
    all_to_all x1, starting transfers between devices, shards(): lax.all_to_all(outgoing, 'seq', split_axis=1, concat_axis=1, tiled=True)  6.08 us
    ppermute x2, starting transfers between devices, padded(): before = lax.ppermute(last, axis, up)  6.07 us
  transfers between devices with their start and end apart: 6, of which 2 were waited for; matrix products, arithmetic and copies ran while one was open for 9% of the time, Pallas kernels for 0%

commit v1 on v0

v1 whole, which is shorter than its diff:
```python
import itertools

import jax
import jax.numpy as jnp
from jax import lax
from jax.experimental import pallas as pl
from jax.experimental.pallas import tpu as pltpu
from jax.sharding import PartitionSpec as P

C = 1536
M = 384
TAPS = 5
STEP = 32
ROWS = 128
SEQ = 8
LENGTH = ROWS * SEQ
EDGE = TAPS // 2 * STEP
CAP = 16
JUNC = 448
PAIR = 2 * CAP
SLOTS = SEQ * PAIR
SIDE = 4
DP = SIDE * SIDE
OWNED = 12
BAND = 16

EPS = 1e-06
SLOPE = 0.7978845608028654
CUBIC = 0.044715

MESH = pl.DeviceIdType.MESH
bf16 = jnp.bfloat16
f32 = jnp.float32
i32 = jnp.int32


def dot(a, b):
    return jnp.dot(a, b, preferred_element_type=f32)


def dot_nt(a, b):
    return lax.dot_general(a, b, (((1,), (1,)), ((), ())), preferred_element_type=f32)


def dot_tn(a, b):
    return lax.dot_general(a, b, (((0,), (0,)), ((), ())), preferred_element_type=f32)


def one_hot(count, row):
    return lax.broadcasted_iota(i32, (count, row.shape[1]), 0) == row


def ones_of(mask):
    return jnp.where(mask, 1.0, 0.0).astype(bf16)


def gelu_parts(v):
    curved = jnp.tanh(SLOPE * (v + CUBIC * v * v * v))
    hidden = 0.5 * v * (1.0 + curved)
    slope = 0.5 * (1.0 + curved) + 0.5 * v * (1.0 - curved * curved) * SLOPE * (
        1.0 + 3.0 * CUBIC * v * v
    )
    return hidden, slope


def junction_matrices(s, don, acc, flags, grad):
    scaled = grad * flags.astype(f32) * C ** (-0.5)
    high = scaled.astype(bf16)
    low = (scaled - high.astype(f32)).astype(bf16)
    don_owner = don >> 7
    acc_owner = acc >> 7
    pairs = ones_of(one_hot(SEQ * SEQ, don_owner * SEQ + acc_owner))
    earlier = ones_of(
        lax.broadcasted_iota(i32, (JUNC, JUNC), 0) < lax.broadcasted_iota(i32, (JUNC, JUNC), 1)
    )
    counts = dot(pairs, earlier)
    rank = jnp.sum(pairs.astype(f32) * counts, axis=0, keepdims=True).astype(i32)
    don_here = don_owner == s
    acc_here = acc_owner == s
    don_at = one_hot(ROWS, don - s * ROWS)
    acc_at = one_hot(ROWS, acc - s * ROWS)
    send_don = ones_of(one_hot(SLOTS, jnp.where(don_here, acc_owner * PAIR + rank, -1)))
    send_acc = ones_of(one_hot(SLOTS, jnp.where(acc_here, don_owner * PAIR + CAP + rank, -1)))
    select = (dot_nt(send_don, ones_of(don_at)) + dot_nt(send_acc, ones_of(acc_at))).astype(bf16)
    came_don = ones_of(one_hot(SLOTS, jnp.where(acc_here, don_owner * PAIR + rank, -1)))
    came_acc = ones_of(one_hot(SLOTS, jnp.where(don_here, acc_owner * PAIR + CAP + rank, -1)))

    def placing(weight):
        wide = weight.astype(f32)
        at_acc = jnp.where(acc_at, wide, 0.0).astype(bf16)
        at_don = jnp.where(don_at, wide, 0.0).astype(bf16)
        return (dot_nt(at_acc, came_don) + dot_nt(at_don, came_acc)).astype(bf16)

    return select, placing(high), placing(low)


def kernel(
    act_hbm,
    w_hbm,
    ow_hbm,
    cot_hbm,
    don_hbm,
    acc_hbm,
    flag_hbm,
    grad_hbm,
    block_hbm,
    input_hbm,
    conv_hbm,
    out_hbm,
    act,
    w,
    ow,
    cot,
    don,
    acc,
    flag,
    grad,
    npad,
    xsend,
    xall,
    gsend,
    grecv,
    hsend,
    hrecv,
    bsend,
    brecv,
    gall,
    cbuf,
    c1,
    c2,
    c3,
    osend,
    osib,
    obuf,
    o1,
    o2,
    o3,
    oz,
    ozr,
    block,
    result,
    cout,
    oout,
    lsem,
    ssem,
    rsem,
):
    s = lax.axis_index("seq")
    d = lax.axis_index("dp")
    z, core = s // 2, s % 2
    y, x = d // SIDE, d % SIDE
    sibling = s + 1 - 2 * core
    ids = itertools.count()
    pending = []

    def push(src, dst, **device):
        i = next(ids)
        copy = pltpu.make_async_remote_copy(
            src_ref=src,
            dst_ref=dst,
            send_sem=ssem.at[i],
            recv_sem=rsem.at[i],
            device_id=device,
            device_id_type=MESH,
        )
        copy.start()
        pending.append(copy)
        return copy

    def seq_at(step):
        return lax.rem(s + step, SEQ)

    def x_at(step):
        return lax.rem(x + step, SIDE)

    def y_at(step):
        return lax.rem(y + step, SIDE)

    loads = {}
    for i, (name, src, dst) in enumerate(
        (
            ("act", act_hbm.at[0], act),
            ("don", don_hbm, don),
            ("acc", acc_hbm, acc),
            ("flag", flag_hbm, flag),
            ("grad", grad_hbm, grad),
            ("ow", ow_hbm, ow),
            ("w", w_hbm, w),
            ("cot", cot_hbm.at[0], cot),
        )
    ):
        loads[name] = pltpu.make_async_copy(src, dst, lsem.at[i])
        loads[name].start()

    barrier = pltpu.get_barrier_semaphore()
    for step in range(1, SEQ):
        pl.semaphore_signal(barrier, inc=1, device_id={"seq": seq_at(step)}, device_id_type=MESH)
    for step in range(1, SIDE):
        pl.semaphore_signal(
            barrier, inc=1, device_id={"dp": y * SIDE + x_at(step)}, device_id_type=MESH
        )
        pl.semaphore_signal(
            barrier, inc=1, device_id={"dp": y_at(step) * SIDE + x}, device_id_type=MESH
        )

    gall[0:EDGE] = jnp.zeros((EDGE, M), bf16)
    gall[EDGE + LENGTH :] = jnp.zeros((EDGE, M), bf16)

    loads["act"].wait()
    act_float = act[...].astype(f32)
    inverse = lax.rsqrt(jnp.mean(act_float * act_float, axis=-1, keepdims=True) + EPS)
    npad[EDGE : EDGE + ROWS] = (act_float * inverse).astype(bf16)
    pl.semaphore_wait(barrier, SEQ - 1 + 2 * (SIDE - 1))
    ahead = push(npad.at[ROWS : ROWS + EDGE], npad.at[0:EDGE], seq=seq_at(1))
    behind = push(npad.at[EDGE : 2 * EDGE], npad.at[EDGE + ROWS :], seq=seq_at(SEQ - 1))

    for name in ("don", "acc", "flag", "grad"):
        loads[name].wait()
    select, place_high, place_low = junction_matrices(s, don[...], acc[...], flag[...], grad[...])

    def own_block(ref):
        return ref.at[pl.ds(pl.multiple_of(s * PAIR, PAIR), PAIR)]

    def send_slots(rows, out, into):
        out[...] = dot(select, rows).astype(bf16)
        own_block(into)[...] = own_block(out)[...]
        copies = []
        for step in (1, 7, 2, 6, 3, 5, 4):
            peer = seq_at(step)
            src = out.at[pl.ds(pl.multiple_of(peer * PAIR, PAIR), PAIR)]
            copies.append(push(src, own_block(into), seq=peer))
        return copies

    def placed(ref):
        return dot(place_high, ref[...]) + dot(place_low, ref[...])

    loads["ow"].wait()
    ow_value = ow[...]
    act_back = dot_nt(act[...], ow_value).astype(bf16)
    act_slots = send_slots(act_back, gsend, grecv)

    loads["w"].wait()
    preact = dot(npad[EDGE : EDGE + ROWS], w[TAPS // 2])
    ahead.wait_recv()
    behind.wait_recv()

    @pl.when(s == 0)
    def _():
        npad[0:EDGE] = jnp.zeros((EDGE, C), bf16)

    @pl.when(s == SEQ - 1)
    def _():
        npad[EDGE + ROWS :] = jnp.zeros((EDGE, C), bf16)

    for tap in (0, 1, 3, 4):
        preact = preact + dot(npad[tap * STEP : tap * STEP + ROWS], w[tap])
    hidden_float, slope = gelu_parts(preact)
    hidden = hidden_float.astype(bf16)
    hidden_slots = send_slots(hidden, hsend, hrecv)

    column = lax.broadcasted_iota(i32, (1, SEQ * ROWS), 1)
    band_row = column % BAND
    wanted = jnp.where(
        band_row < OWNED,
        (column % ROWS) // BAND * (OWNED * SEQ) + column // ROWS * OWNED + band_row,
        -1,
    )
    regroup = ones_of(one_hot(C // 2, wanted))
    for half in range(2):
        part = dot(npad[EDGE : EDGE + ROWS, half * (C // 2) : (half + 1) * (C // 2)], regroup)
        for peer in range(SEQ):
            xsend[peer, :, half * ROWS : (half + 1) * ROWS] = part[
                :, peer * ROWS : (peer + 1) * ROWS
            ].astype(bf16)
    here = pl.ds(pl.multiple_of(s * ROWS, ROWS), ROWS)
    xall[here] = xsend[s]
    x_copies = [
        push(xsend.at[seq_at(step)], xall.at[here], seq=seq_at(step))
        for step in (1, 7, 2, 6, 3, 5, 4)
    ]

    block[...] = (act[...].astype(f32) + dot(hidden, ow_value)).astype(bf16)
    block_store = pltpu.make_async_copy(block, block_hbm.at[0], lsem.at[8])
    block_store.start()
    loads["cot"].wait()
    cot_back = dot_nt(cot[...], ow_value)
    ow_square = dot_nt(ow_value, ow_value).astype(bf16)

    for copy in act_slots:
        copy.wait_recv()
    cot_back = cot_back + placed(grecv)
    for copy in hidden_slots:
        copy.wait_recv()
    mixed = placed(hrecv).astype(bf16)
    grad_hidden = cot_back + dot(mixed, ow_square)
    grad_here = pl.ds(pl.multiple_of(EDGE + s * ROWS, EDGE), ROWS)
    gall[grad_here] = (grad_hidden * slope).astype(bf16)

    def chunk(owner):
        return gall.at[pl.ds(pl.multiple_of(EDGE + owner * ROWS, EDGE), ROWS)]

    along = [push(chunk(s), chunk(s), seq=seq_at(2 * step)) for step in (1, 3, 2)]
    across = [push(chunk(s), chunk(s), seq=sibling)]

    slot = lax.broadcasted_iota(i32, (1, 2 * DP * BAND), 1)
    within = slot % BAND
    third = (within * 11) >> 5
    wanted = jnp.where(
        within < OWNED,
        (slot % (DP * BAND)) // BAND * (3 * SEQ)
        + third * 6
        + slot // (DP * BAND) * 3
        + within
        - third * 3,
        -1,
    )
    order = ones_of(one_hot(M, wanted))
    hidden_order = dot(hidden, order).astype(bf16)
    mixed_order = dot(mixed, order).astype(bf16)
    terms = dot_tn(hidden_order, cot[...]) + dot_tn(mixed_order, block[...])
    osend[...] = terms.astype(bf16).reshape(2, SIDE, SIDE, BAND, C)
    to_sibling = push(osend.at[1 - core], osib, seq=sibling)

    for step, copy in zip((1, 3, 2), along):
        copy.wait_recv()
        owner = lax.rem(s + SEQ - 2 * step, SEQ)
        across.append(push(chunk(owner), chunk(owner), seq=sibling))

    block_slots = send_slots(block[...], bsend, brecv)

    to_sibling.wait_recv()
    obuf[...] = (osend[core].astype(f32) + osib[...].astype(f32)).astype(bf16)
    out_first = [
        push(obuf.at[y_at(step)], o1.at[step - 1], dp=y_at(step) * SIDE + x)
        for step in range(1, SIDE)
    ]

    for copy in x_copies:
        copy.wait_recv()
    for copy in across:
        copy.wait_recv()

    conv_first = []
    for tap in range(TAPS):
        start = 2 * EDGE - tap * STEP
        term = dot_tn(xall[...], gall[start : start + LENGTH])
        cbuf[tap] = term.astype(bf16).reshape(SIDE, SIDE, BAND, M)
        copies = []
        for step in range(1, SIDE):
            if tap % 2 == 0:
                copies.append(
                    push(
                        cbuf.at[tap, :, x_at(step)],
                        c1.at[tap, step - 1],
                        dp=y * SIDE + x_at(step),
                    )
                )
            else:
                copies.append(
                    push(
                        cbuf.at[tap, y_at(step)],
                        c1.at[tap, step - 1],
                        dp=y_at(step) * SIDE + x,
                    )
                )
        conv_first.append(copies)

    for copy in out_first:
        copy.wait_recv()
    total = obuf[y].astype(f32)
    for step in range(1, SIDE):
        total = total + o1[step - 1].astype(f32)
    o2[...] = total.astype(bf16)
    out_second = [
        push(o2.at[x_at(step)], o3.at[step - 1], dp=y * SIDE + x_at(step))
        for step in range(1, SIDE)
    ]

    grad_normed = jnp.zeros((ROWS, C), f32)
    conv_second = []
    for tap in range(TAPS):
        start = pl.multiple_of(s * ROWS + 2 * EDGE - tap * STEP, STEP)
        grad_normed = grad_normed + dot_nt(gall[pl.ds(start, ROWS)], w[tap])
        for copy in conv_first[tap]:
            copy.wait_recv()
        own = cbuf[tap, :, x] if tap % 2 == 0 else cbuf[tap, y]
        total = own.astype(f32)
        for step in range(1, SIDE):
            total = total + c1[tap, step - 1].astype(f32)
        c2[tap] = total.astype(bf16)
        copies = []
        for step in range(1, SIDE):
            if tap % 2 == 0:
                copies.append(
                    push(
                        c2.at[tap, y_at(step)],
                        c3.at[tap, step - 1],
                        dp=y_at(step) * SIDE + x,
                    )
                )
            else:
                copies.append(
                    push(
                        c2.at[tap, x_at(step)],
                        c3.at[tap, step - 1],
                        dp=y * SIDE + x_at(step),
                    )
                )
        conv_second.append(copies)

    for copy in out_second:
        copy.wait_recv()
    total = o2[x].astype(f32)
    for step in range(1, SIDE):
        total = total + o3[step - 1].astype(f32)
    oz[...] = total.astype(bf16)
    out_third = [
        push(oz, ozr.at[step - 1], seq=seq_at(2 * step)) for step in range(1, SIDE)
    ]

    for copy in block_slots:
        copy.wait_recv()
    act_float = act[...].astype(f32)
    upstream = (cot[...].astype(f32) + placed(brecv)).astype(bf16)
    spread = jnp.mean(grad_normed * act_float, axis=-1, keepdims=True)
    result[...] = (
        upstream.astype(f32)
        + inverse * grad_normed
        - inverse * inverse * inverse * act_float * spread
    ).astype(bf16)
    input_store = pltpu.make_async_copy(result, input_hbm.at[0], lsem.at[9])
    input_store.start()

    for tap in range(TAPS):
        for copy in conv_second[tap]:
            copy.wait_recv()
        total = (c2[tap, y] if tap % 2 == 0 else c2[tap, x]).astype(f32)
        for step in range(1, SIDE):
            total = total + c3[tap, step - 1].astype(f32)
        cout[tap] = total[:OWNED]
    conv_store = pltpu.make_async_copy(cout, conv_hbm, lsem.at[10])
    conv_store.start()

    for copy in out_third:
        copy.wait_recv()
    total = oz[...].astype(f32)
    for step in range(1, SIDE):
        total = total + ozr[step - 1].astype(f32)
    rows = total[0:3]
    for level in range(1, SIDE):
        rows = jnp.where(z == level, total[3 * level : 3 * level + 3], rows)
    oout[...] = rows
    out_store = pltpu.make_async_copy(oout, out_hbm, lsem.at[11])
    out_store.start()

    for copy in pending:
        copy.wait_send()
    for store in (block_store, input_store, conv_store, out_store):
        store.wait()


COPIES = 2 + 7 + 7 + 7 + 7 + 3 + 4 + 1 + 3 + 15 + 3 + 15 + 3


def shards(act, w, ow, cot, don, acc, flag, grad):
    any_space = pl.BlockSpec(memory_space=pl.ANY)
    vmem = pltpu.VMEM
    return pl.pallas_call(
        kernel,
        name="block_step",
        out_shape=(
            jax.ShapeDtypeStruct((1, ROWS, C), bf16),
            jax.ShapeDtypeStruct((1, ROWS, C), bf16),
            jax.ShapeDtypeStruct((TAPS, OWNED, M), f32),
            jax.ShapeDtypeStruct((3, C), f32),
        ),
        in_specs=[any_space] * 8,
        out_specs=[any_space] * 4,
        scratch_shapes=[
            vmem((ROWS, C), bf16),
            vmem((TAPS, C, M), bf16),
            vmem((M, C), bf16),
            vmem((ROWS, C), bf16),
            vmem((1, JUNC), i32),
            vmem((1, JUNC), i32),
            vmem((1, JUNC), i32),
            vmem((1, JUNC), f32),
            vmem((ROWS + 2 * EDGE, C), bf16),
            vmem((SEQ, ROWS, DP * BAND), bf16),
            vmem((LENGTH, DP * BAND), bf16),
            vmem((SLOTS, M), bf16),
            vmem((SLOTS, M), bf16),
            vmem((SLOTS, M), bf16),
            vmem((SLOTS, M), bf16),
            vmem((SLOTS, C), bf16),
            vmem((SLOTS, C), bf16),
            vmem((LENGTH + 2 * EDGE, M), bf16),
            vmem((TAPS, SIDE, SIDE, BAND, M), bf16),
            vmem((TAPS, SIDE - 1, SIDE, BAND, M), bf16),
            vmem((TAPS, SIDE, BAND, M), bf16),
            vmem((TAPS, SIDE - 1, BAND, M), bf16),
            vmem((2, SIDE, SIDE, BAND, C), bf16),
            vmem((SIDE, SIDE, BAND, C), bf16),
            vmem((SIDE, SIDE, BAND, C), bf16),
            vmem((SIDE - 1, SIDE, BAND, C), bf16),
            vmem((SIDE, BAND, C), bf16),
            vmem((SIDE - 1, BAND, C), bf16),
            vmem((BAND, C), bf16),
            vmem((SIDE - 1, BAND, C), bf16),
            vmem((ROWS, C), bf16),
            vmem((ROWS, C), bf16),
            vmem((TAPS, OWNED, M), f32),
            vmem((3, C), f32),
            pltpu.SemaphoreType.DMA((12,)),
            pltpu.SemaphoreType.DMA((COPIES,)),
            pltpu.SemaphoreType.DMA((COPIES,)),
        ],
        compiler_params=pltpu.CompilerParams(
            collective_id=0, has_side_effects=True, vmem_limit_bytes=56 * 1024 * 1024
        ),
    )(act, w, ow, cot, don, acc, flag, grad)


def solution(mesh):
    in_specs = (
        P("dp", "seq", None),
        P(),
        P(),
        P("dp", "seq", None),
        P("dp", None),
        P("dp", None),
        P("dp", None),
        P("dp", None),
    )
    out_specs = (
        P("dp", "seq", None),
        P("dp", "seq", None),
        P(None, ("dp", "seq"), None),
        P(("dp", "seq"), None),
    )
    return jax.shard_map(shards, mesh=mesh, in_specs=in_specs, out_specs=out_specs, check_vma=False)
```

time: 254 us -> 58.7 us (0.23)
  waiting for transfers between devices: 168 us -> 0 us
  Pallas kernels: 0 us -> 51.3 us
  matrix products: 33.5 us -> 0 us
  starting transfers between devices: 14.8 us -> 0 us
  between operations: 14.4 us -> 0.64 us
  other arithmetic: 13.7 us -> 0 us
    unnamed x2 -> x0, waiting for transfers between devices: 157 us -> none
    pallas_call x0 -> x1, Pallas kernels: none -> 51.3 us  [shards(): pl.pallas_call(kernel, name='block_step', out_shape=(jax.ShapeDtypeStruct...]
    dot_general x20 -> x0, matrix products: 33.5 us -> none  [the longest x5 9.65 us: shards(): jnp.einsum('bpc,bpm->cm', sliding_window, preactivation_gradient, preferr...]
    all_to_all x1 -> x0, waiting for transfers between devices: 10.9 us -> none  [shards(): lax.all_to_all(outgoing, 'seq', split_axis=1, concat_axis=1, tiled=True)]
    ppermute x4 -> x0, starting transfers between devices: 8.66 us -> none  [the longest x2 6.07 us: padded(): before = lax.ppermute(last, axis, up)]
    all_to_all x1 -> x0, starting transfers between devices: 6.08 us -> none  [shards(): lax.all_to_all(outgoing, 'seq', split_axis=1, concat_axis=1, tiled=True)]
    gather x4 -> x0, local copies, waits for them, and re-layouts: 3.81 us -> none  [pick_rows(): jnp.take(sequence_rows, row_index, axis=0)]
    reduce_sum x5 -> x0, other arithmetic: 3.56 us -> none  [the longest x1 1.55 us: junction_slots(): accept_coef = jnp.sum(jnp.where(accept_hit, scaled[:, None], 0.0), axis=0)]
  transfers between devices with their start and end apart: 6 -> 0, of which waited for: 2 -> 0; matrix products, arithmetic and copies ran while one was open for 9% -> 0% of each run, Pallas kernels for 0% -> 0%
where the time goes in v1:
time: 58.7 us; the launch traced here: 58.4 us
  Pallas kernels  51.3 us (87%)
  local copies, waits for them, and re-layouts  6.44 us (11%)
  between operations  0.64 us (1%)
    pallas_call x1, Pallas kernels, shards(): pl.pallas_call(kernel, name='block_step', out_shape=(jax.ShapeDtypeStruct...  51.3 us
    unnamed x4, local copies, waits for them, and re-layouts  6.44 us

profile of v1, /device:TPU:0, one launch (start us, length us, event | category | flops | bytes accessed | tf_op | source)
XLA Modules:
  0.0 58.4 jit_solution(10536919527376498)
XLA Ops:
  0.6 51.3 %block_step.1 = (bf16[1,128,1536]{2,1,0:T(8,128)(2,1)}, bf16[1,128,1536]{2,1,0:T(8,128)(2,1)}, f32[5,12,384]{2,1,0:T(8,128)}, f32[3,1536]{1,0:T(4,128)}) custom-call(bf16[1,128,1536]{2,1,0:T(8,128)(2,1)} %act_hbm.1, bf16[5,1536,384]{2,1,0:T(8,128)(2,1)} %w_hbm.1, bf16[384,1536]{1,0:T(8,128)(2,1)} %ow_hbm.1, bf16[1,128,1536]{2,1,0:T(8,128)(2,1)} %cot_hbm.1, ...), custom_call_target="tpu_custom_call" | custom-call | tf_op jit(solution)/shard_map/block_step/pallas_call | solution.py:468
  51.9 1.8 %copy.16 = bf16[1,128,1536]{2,1,0:T(8,128)(2,1)} copy(bf16[1,128,1536]{2,1,0:T(8,128)(2,1)} %get-tuple-element.8) | data formatting | bytes 786432
  53.7 1.8 %copy.17 = bf16[1,128,1536]{2,1,0:T(8,128)(2,1)} copy(bf16[1,128,1536]{2,1,0:T(8,128)(2,1)} %get-tuple-element.9) | data formatting | bytes 786432
  55.5 1.6 %copy.18 = f32[5,12,384]{2,1,0:T(8,128)} copy(f32[5,12,384]{2,1,0:T(8,128)} %get-tuple-element.10) | data formatting | bytes 184320
  57.0 1.3 %copy.19 = f32[3,1536]{1,0:T(4,128)} copy(f32[3,1536]{1,0:T(4,128)} %get-tuple-element.11) | data formatting | bytes 36864

commit v2 on v1

--- a/solution.py
+++ b/solution.py
@@ -23,6 +23,12 @@
 DP = SIDE * SIDE
 OWNED = 12
 BAND = 16
+SHARE = DP * OWNED
+YPART = 1024
+
+TAP_ORDER = (0, 1, 4, 3, 2)
+NEAR = (1, 7, 2, 6, 3, 5, 4)
+X_EARLY = 7
 
 EPS = 1e-06
 SLOPE = 0.7978845608028654
@@ -115,9 +121,12 @@
     acc,
     flag,
     grad,
-    npad,
+    edge_send,
+    edge_recv,
     xsend,
     xall,
+    xy_order,
+    xx_order,
     gsend,
     grecv,
     hsend,
@@ -129,12 +138,18 @@
     c1,
     c2,
     c3,
-    osend,
-    osib,
-    obuf,
-    o1,
-    o2,
-    o3,
+    osend_y,
+    osend_x,
+    osib_y,
+    osib_x,
+    obuf_y,
+    obuf_x,
+    o1_y,
+    o1_x,
+    o2_y,
+    o2_x,
+    o3_y,
+    o3_x,
     oz,
     ozr,
     block,
@@ -184,8 +199,8 @@
             ("acc", acc_hbm, acc),
             ("flag", flag_hbm, flag),
             ("grad", grad_hbm, grad),
+            *((f"w{tap}", w_hbm.at[tap], w.at[tap]) for tap in TAP_ORDER),
             ("ow", ow_hbm, ow),
-            ("w", w_hbm, w),
             ("cot", cot_hbm.at[0], cot),
         )
     ):
@@ -209,11 +224,42 @@
     loads["act"].wait()
     act_float = act[...].astype(f32)
     inverse = lax.rsqrt(jnp.mean(act_float * act_float, axis=-1, keepdims=True) + EPS)
-    npad[EDGE : EDGE + ROWS] = (act_float * inverse).astype(bf16)
+    normed = (act_float * inverse).astype(bf16)
+
+    column = lax.broadcasted_iota(i32, (1, C), 1)
+    owner, lane = column // SHARE, column % SHARE
+    regroup = ones_of(one_hot(C, lane // OWNED * (OWNED * SEQ) + owner * OWNED + lane % OWNED))
+    grouped = dot(normed, regroup)
+    left = lax.broadcasted_iota(i32, (ROWS // 2, 2 * SHARE), 1) < SHARE
+    for pair in range(SEQ // 2):
+        both = grouped[:, pair * 2 * SHARE : (pair + 1) * 2 * SHARE]
+        upper, lower = both[: ROWS // 2], both[ROWS // 2 :]
+        xsend[2 * pair] = jnp.where(left, upper, pltpu.roll(lower, SHARE, 1)).astype(bf16)
+        xsend[2 * pair + 1] = jnp.where(left, pltpu.roll(upper, SHARE, 1), lower).astype(bf16)
+    xall[s] = xsend[s]
     pl.semaphore_wait(barrier, SEQ - 1 + 2 * (SIDE - 1))
-    ahead = push(npad.at[ROWS : ROWS + EDGE], npad.at[0:EDGE], seq=seq_at(1))
-    behind = push(npad.at[EDGE : 2 * EDGE], npad.at[EDGE + ROWS :], seq=seq_at(SEQ - 1))
-
+
+    def send_channels(steps):
+        return [push(xsend.at[seq_at(step)], xall.at[s], seq=seq_at(step)) for step in steps]
+
+    x_copies = send_channels(NEAR[:X_EARLY])
+
+    taps = {}
+    for tap in (0, 1):
+        loads[f"w{tap}"].wait()
+        taps[tap] = dot(normed, w[tap])
+    half = ROWS // 2
+    edge_send[0] = (
+        taps[0][half:] + jnp.concatenate([taps[1][ROWS - STEP :], jnp.zeros((STEP, M), f32)], axis=0)
+    ).astype(bf16)
+    ahead = push(edge_send.at[0], edge_recv.at[0], seq=seq_at(1))
+    for tap in (4, 3):
+        loads[f"w{tap}"].wait()
+        taps[tap] = dot(normed, w[tap])
+    edge_send[1] = (
+        taps[4][:half] + jnp.concatenate([jnp.zeros((STEP, M), f32), taps[3][:STEP]], axis=0)
+    ).astype(bf16)
+    behind = push(edge_send.at[1], edge_recv.at[1], seq=seq_at(SEQ - 1))
     for name in ("don", "acc", "flag", "grad"):
         loads[name].wait()
     select, place_high, place_low = junction_matrices(s, don[...], acc[...], flag[...], grad[...])
@@ -225,7 +271,7 @@
         out[...] = dot(select, rows).astype(bf16)
         own_block(into)[...] = own_block(out)[...]
         copies = []
-        for step in (1, 7, 2, 6, 3, 5, 4):
+        for step in NEAR:
             peer = seq_at(step)
             src = out.at[pl.ds(pl.multiple_of(peer * PAIR, PAIR), PAIR)]
             copies.append(push(src, own_block(into), seq=peer))
@@ -239,48 +285,42 @@
     act_back = dot_nt(act[...], ow_value).astype(bf16)
     act_slots = send_slots(act_back, gsend, grecv)
 
-    loads["w"].wait()
-    preact = dot(npad[EDGE : EDGE + ROWS], w[TAPS // 2])
+    loads["w2"].wait()
+    preact = dot(normed, w[2])
+    preact = preact + jnp.concatenate(
+        [
+            taps[4][half:] + taps[3][STEP : STEP + half],
+            jnp.concatenate([taps[3][STEP + half :], jnp.zeros((STEP, M), f32)], axis=0)
+            + taps[0][:half]
+            + taps[1][STEP : STEP + half],
+        ],
+        axis=0,
+    )
+    preact = preact + jnp.concatenate(
+        [
+            jnp.zeros((STEP, M), f32),
+            taps[1][:STEP],
+            jnp.zeros((half, M), f32),
+        ],
+        axis=0,
+    )
     ahead.wait_recv()
     behind.wait_recv()
-
-    @pl.when(s == 0)
-    def _():
-        npad[0:EDGE] = jnp.zeros((EDGE, C), bf16)
-
-    @pl.when(s == SEQ - 1)
-    def _():
-        npad[EDGE + ROWS :] = jnp.zeros((EDGE, C), bf16)
-
-    for tap in (0, 1, 3, 4):
-        preact = preact + dot(npad[tap * STEP : tap * STEP + ROWS], w[tap])
+    preact = preact + jnp.concatenate(
+        [
+            jnp.where(s > 0, edge_recv[0].astype(f32), 0.0),
+            jnp.where(s < SEQ - 1, edge_recv[1].astype(f32), 0.0),
+        ],
+        axis=0,
+    )
     hidden_float, slope = gelu_parts(preact)
     hidden = hidden_float.astype(bf16)
     hidden_slots = send_slots(hidden, hsend, hrecv)
 
-    column = lax.broadcasted_iota(i32, (1, SEQ * ROWS), 1)
-    band_row = column % BAND
-    wanted = jnp.where(
-        band_row < OWNED,
-        (column % ROWS) // BAND * (OWNED * SEQ) + column // ROWS * OWNED + band_row,
-        -1,
-    )
-    regroup = ones_of(one_hot(C // 2, wanted))
-    for half in range(2):
-        part = dot(npad[EDGE : EDGE + ROWS, half * (C // 2) : (half + 1) * (C // 2)], regroup)
-        for peer in range(SEQ):
-            xsend[peer, :, half * ROWS : (half + 1) * ROWS] = part[
-                :, peer * ROWS : (peer + 1) * ROWS
-            ].astype(bf16)
-    here = pl.ds(pl.multiple_of(s * ROWS, ROWS), ROWS)
-    xall[here] = xsend[s]
-    x_copies = [
-        push(xsend.at[seq_at(step)], xall.at[here], seq=seq_at(step))
-        for step in (1, 7, 2, 6, 3, 5, 4)
-    ]
+    x_copies += send_channels(NEAR[X_EARLY:])
 
     block[...] = (act[...].astype(f32) + dot(hidden, ow_value)).astype(bf16)
-    block_store = pltpu.make_async_copy(block, block_hbm.at[0], lsem.at[8])
+    block_store = pltpu.make_async_copy(block, block_hbm.at[0], lsem.at[12])
     block_store.start()
     loads["cot"].wait()
     cot_back = dot_nt(cot[...], ow_value)
@@ -302,24 +342,35 @@
     along = [push(chunk(s), chunk(s), seq=seq_at(2 * step)) for step in (1, 3, 2)]
     across = [push(chunk(s), chunk(s), seq=sibling)]
 
-    slot = lax.broadcasted_iota(i32, (1, 2 * DP * BAND), 1)
-    within = slot % BAND
-    third = (within * 11) >> 5
-    wanted = jnp.where(
-        within < OWNED,
-        (slot % (DP * BAND)) // BAND * (3 * SEQ)
-        + third * 6
-        + slot // (DP * BAND) * 3
-        + within
-        - third * 3,
-        -1,
-    )
-    order = ones_of(one_hot(M, wanted))
-    hidden_order = dot(hidden, order).astype(bf16)
-    mixed_order = dot(mixed, order).astype(bf16)
-    terms = dot_tn(hidden_order, cot[...]) + dot_tn(mixed_order, block[...])
-    osend[...] = terms.astype(bf16).reshape(2, SIDE, SIDE, BAND, C)
-    to_sibling = push(osend.at[1 - core], osib, seq=sibling)
+    def ordered(first):
+        lane = lax.broadcasted_iota(i32, (1, M), 1)
+        half, rest = lane // (DP * OWNED), lane % (DP * OWNED)
+        outer, rest = rest // (SIDE * OWNED), rest % (SIDE * OWNED)
+        inner, rest = rest // OWNED, rest % OWNED
+        device = outer * SIDE + inner if first == "y" else inner * SIDE + outer
+        order = ones_of(one_hot(M, device * 3 * SEQ + rest // 3 * 6 + half * 3 + rest % 3))
+        return dot(hidden, order).astype(bf16), dot(mixed, order).astype(bf16)
+
+    def out_terms(first, columns):
+        hidden_order, mixed_order = ordered(first)
+        terms = dot_tn(hidden_order, cot[:, columns]) + dot_tn(mixed_order, block[:, columns])
+        return terms.astype(bf16).reshape(2, SIDE, SIDE * OWNED, columns.stop - columns.start)
+
+    osend_y[...] = out_terms("y", slice(0, YPART))
+    osend_x[...] = out_terms("x", slice(YPART, C))
+    to_sibling = [
+        push(osend_y.at[1 - core], osib_y, seq=sibling),
+        push(osend_x.at[1 - core], osib_x, seq=sibling),
+    ]
+
+    for copy in to_sibling:
+        copy.wait_recv()
+    obuf_y[...] = (osend_y[core].astype(f32) + osib_y[...].astype(f32)).astype(bf16)
+    obuf_x[...] = (osend_x[core].astype(f32) + osib_x[...].astype(f32)).astype(bf16)
+    out_first = []
+    for step in range(1, SIDE):
+        out_first.append(push(obuf_y.at[y_at(step)], o1_y.at[step - 1], dp=y_at(step) * SIDE + x))
+        out_first.append(push(obuf_x.at[x_at(step)], o1_x.at[step - 1], dp=y * SIDE + x_at(step)))
 
     for step, copy in zip((1, 3, 2), along):
         copy.wait_recv()
@@ -328,53 +379,64 @@
 
     block_slots = send_slots(block[...], bsend, brecv)
 
-    to_sibling.wait_recv()
-    obuf[...] = (osend[core].astype(f32) + osib[...].astype(f32)).astype(bf16)
-    out_first = [
-        push(obuf.at[y_at(step)], o1.at[step - 1], dp=y_at(step) * SIDE + x)
-        for step in range(1, SIDE)
-    ]
+    def channels(first):
+        lane = lax.broadcasted_iota(i32, (1, SHARE), 1)
+        outer, rest = lane // (SIDE * OWNED), lane % (SIDE * OWNED)
+        inner, row = rest // OWNED, rest % OWNED
+        device = outer * SIDE + inner if first == "y" else inner * SIDE + outer
+        parts = [
+            dot(came, ones_of(one_hot(2 * SHARE, device * OWNED + row + SHARE * lower)))
+            for lower in range(2)
+        ]
+        parts = [part.astype(bf16).reshape(SEQ, ROWS // 2, SHARE) for part in parts]
+        return jnp.concatenate(parts, axis=1).reshape(LENGTH, SHARE)
 
     for copy in x_copies:
         copy.wait_recv()
+    came = xall[...].reshape(SEQ * ROWS // 2, 2 * SHARE)
+    xy_order[...] = channels("y")
+    xx_order[...] = channels("x")
+
     for copy in across:
         copy.wait_recv()
 
     conv_first = []
     for tap in range(TAPS):
         start = 2 * EDGE - tap * STEP
-        term = dot_tn(xall[...], gall[start : start + LENGTH])
-        cbuf[tap] = term.astype(bf16).reshape(SIDE, SIDE, BAND, M)
+        order = xx_order if tap % 2 == 0 else xy_order
+        term = dot_tn(order[...], gall[start : start + LENGTH])
+        cbuf[tap] = term.astype(bf16).reshape(SIDE, SIDE * OWNED, M)
         copies = []
         for step in range(1, SIDE):
             if tap % 2 == 0:
-                copies.append(
-                    push(
-                        cbuf.at[tap, :, x_at(step)],
-                        c1.at[tap, step - 1],
-                        dp=y * SIDE + x_at(step),
-                    )
-                )
+                at, peer = x_at(step), y * SIDE + x_at(step)
             else:
-                copies.append(
-                    push(
-                        cbuf.at[tap, y_at(step)],
-                        c1.at[tap, step - 1],
-                        dp=y_at(step) * SIDE + x,
-                    )
-                )
+                at, peer = y_at(step), y_at(step) * SIDE + x
+            copies.append(push(cbuf.at[tap, at], c1.at[tap, step - 1], dp=peer))
         conv_first.append(copies)
 
+    band = lax.broadcasted_iota(i32, (SIDE * BAND, SIDE * OWNED), 0)
+    packed = lax.broadcasted_iota(i32, (SIDE * BAND, SIDE * OWNED), 1)
+    spread_rows = ones_of((band // BAND * OWNED + band % BAND == packed) & (band % BAND < OWNED))
+
+    def summed(own, came):
+        total = own.astype(f32)
+        for step in range(1, SIDE):
+            total = total + came[step - 1].astype(f32)
+        return total
+
+    def banded(total):
+        bands = dot(spread_rows, total.astype(bf16)).astype(bf16)
+        return bands.reshape(SIDE, BAND, total.shape[1])
+
     for copy in out_first:
         copy.wait_recv()
-    total = obuf[y].astype(f32)
+    o2_y[...] = banded(summed(obuf_y[y], o1_y))
+    o2_x[...] = banded(summed(obuf_x[x], o1_x))
+    out_second = []
     for step in range(1, SIDE):
-        total = total + o1[step - 1].astype(f32)
-    o2[...] = total.astype(bf16)
-    out_second = [
-        push(o2.at[x_at(step)], o3.at[step - 1], dp=y * SIDE + x_at(step))
-        for step in range(1, SIDE)
-    ]
+        out_second.append(push(o2_y.at[x_at(step)], o3_y.at[step - 1], dp=y * SIDE + x_at(step)))
+        out_second.append(push(o2_x.at[y_at(step)], o3_x.at[step - 1], dp=y_at(step) * SIDE + x))
 
     grad_normed = jnp.zeros((ROWS, C), f32)
     conv_second = []
@@ -383,37 +445,21 @@
         grad_normed = grad_normed + dot_nt(gall[pl.ds(start, ROWS)], w[tap])
         for copy in conv_first[tap]:
             copy.wait_recv()
-        own = cbuf[tap, :, x] if tap % 2 == 0 else cbuf[tap, y]
-        total = own.astype(f32)
-        for step in range(1, SIDE):
-            total = total + c1[tap, step - 1].astype(f32)
-        c2[tap] = total.astype(bf16)
+        own = cbuf[tap, x] if tap % 2 == 0 else cbuf[tap, y]
+        c2[tap] = banded(summed(own, c1.at[tap]))
         copies = []
         for step in range(1, SIDE):
             if tap % 2 == 0:
-                copies.append(
-                    push(
-                        c2.at[tap, y_at(step)],
-                        c3.at[tap, step - 1],
-                        dp=y_at(step) * SIDE + x,
-                    )
-                )
+                at, peer = y_at(step), y_at(step) * SIDE + x
             else:
-                copies.append(
-                    push(
-                        c2.at[tap, x_at(step)],
-                        c3.at[tap, step - 1],
-                        dp=y * SIDE + x_at(step),
-                    )
-                )
+                at, peer = x_at(step), y * SIDE + x_at(step)
+            copies.append(push(c2.at[tap, at], c3.at[tap, step - 1], dp=peer))
         conv_second.append(copies)
 
     for copy in out_second:
         copy.wait_recv()
-    total = o2[x].astype(f32)
-    for step in range(1, SIDE):
-        total = total + o3[step - 1].astype(f32)
-    oz[...] = total.astype(bf16)
+    oz[:, :YPART] = summed(o2_y[x], o3_y).astype(bf16)
+    oz[:, YPART:] = summed(o2_x[y], o3_x).astype(bf16)
     out_third = [
         push(oz, ozr.at[step - 1], seq=seq_at(2 * step)) for step in range(1, SIDE)
     ]
@@ -428,29 +474,25 @@
         + inverse * grad_normed
         - inverse * inverse * inverse * act_float * spread
     ).astype(bf16)
-    input_store = pltpu.make_async_copy(result, input_hbm.at[0], lsem.at[9])
+    input_store = pltpu.make_async_copy(result, input_hbm.at[0], lsem.at[13])
     input_store.start()
 
     for tap in range(TAPS):
         for copy in conv_second[tap]:
             copy.wait_recv()
-        total = (c2[tap, y] if tap % 2 == 0 else c2[tap, x]).astype(f32)
-        for step in range(1, SIDE):
-            total = total + c3[tap, step - 1].astype(f32)
+        total = summed(c2[tap, y] if tap % 2 == 0 else c2[tap, x], c3.at[tap])
         cout[tap] = total[:OWNED]
-    conv_store = pltpu.make_async_copy(cout, conv_hbm, lsem.at[10])
+    conv_store = pltpu.make_async_copy(cout, conv_hbm, lsem.at[14])
     conv_store.start()
 
     for copy in out_third:
         copy.wait_recv()
-    total = oz[...].astype(f32)
-    for step in range(1, SIDE):
-        total = total + ozr[step - 1].astype(f32)
+    total = summed(oz[...], ozr)
     rows = total[0:3]
     for level in range(1, SIDE):
         rows = jnp.where(z == level, total[3 * level : 3 * level + 3], rows)
     oout[...] = rows
-    out_store = pltpu.make_async_copy(oout, out_hbm, lsem.at[11])
+    out_store = pltpu.make_async_copy(oout, out_hbm, lsem.at[15])
     out_store.start()
 
     for copy in pending:
@@ -459,21 +501,37 @@
         store.wait()
 
 
-COPIES = 2 + 7 + 7 + 7 + 7 + 3 + 4 + 1 + 3 + 15 + 3 + 15 + 3
+COPIES = 2 + 7 + 7 + 7 + 7 + 3 + 4 + 2 + 6 + 15 + 6 + 15 + 3
+
+
+def store_kernel(*refs):
+    came, left, held, sem = refs[:4], refs[4:8], refs[8:12], refs[12]
+    loads = [pltpu.make_async_copy(came[i], held[i], sem.at[i]) for i in range(4)]
+    stores = [pltpu.make_async_copy(held[i], left[i], sem.at[4 + i]) for i in range(4)]
+    for load in loads:
+        load.start()
+    for load, store in zip(loads, stores):
+        load.wait()
+        store.start()
+    for store in stores:
+        store.wait()
+
+
+OUTPUTS = (
+    jax.ShapeDtypeStruct((1, ROWS, C), bf16),
+    jax.ShapeDtypeStruct((1, ROWS, C), bf16),
+    jax.ShapeDtypeStruct((TAPS, OWNED, M), f32),
+    jax.ShapeDtypeStruct((3, C), f32),
+)
 
 
 def shards(act, w, ow, cot, don, acc, flag, grad):
     any_space = pl.BlockSpec(memory_space=pl.ANY)
     vmem = pltpu.VMEM
-    return pl.pallas_call(
+    results = pl.pallas_call(
         kernel,
         name="block_step",
-        out_shape=(
-            jax.ShapeDtypeStruct((1, ROWS, C), bf16),
-            jax.ShapeDtypeStruct((1, ROWS, C), bf16),
-            jax.ShapeDtypeStruct((TAPS, OWNED, M), f32),
-            jax.ShapeDtypeStruct((3, C), f32),
-        ),
+        out_shape=OUTPUTS,
         in_specs=[any_space] * 8,
         out_specs=[any_space] * 4,
         scratch_shapes=[
@@ -485,9 +543,12 @@
             vmem((1, JUNC), i32),
             vmem((1, JUNC), i32),
             vmem((1, JUNC), f32),
-            vmem((ROWS + 2 * EDGE, C), bf16),
-            vmem((SEQ, ROWS, DP * BAND), bf16),
-            vmem((LENGTH, DP * BAND), bf16),
+            vmem((2, EDGE, M), bf16),
+            vmem((2, EDGE, M), bf16),
+            vmem((SEQ, ROWS // 2, 2 * SHARE), bf16),
+            vmem((SEQ, ROWS // 2, 2 * SHARE), bf16),
+            vmem((LENGTH, SHARE), bf16),
+            vmem((LENGTH, SHARE), bf16),
             vmem((SLOTS, M), bf16),
             vmem((SLOTS, M), bf16),
             vmem((SLOTS, M), bf16),
@@ -495,23 +556,29 @@
             vmem((SLOTS, C), bf16),
             vmem((SLOTS, C), bf16),
             vmem((LENGTH + 2 * EDGE, M), bf16),
-            vmem((TAPS, SIDE, SIDE, BAND, M), bf16),
-            vmem((TAPS, SIDE - 1, SIDE, BAND, M), bf16),
+            vmem((TAPS, SIDE, SIDE * OWNED, M), bf16),
+            vmem((TAPS, SIDE - 1, SIDE * OWNED, M), bf16),
             vmem((TAPS, SIDE, BAND, M), bf16),
             vmem((TAPS, SIDE - 1, BAND, M), bf16),
-            vmem((2, SIDE, SIDE, BAND, C), bf16),
-            vmem((SIDE, SIDE, BAND, C), bf16),
-            vmem((SIDE, SIDE, BAND, C), bf16),
-            vmem((SIDE - 1, SIDE, BAND, C), bf16),
-            vmem((SIDE, BAND, C), bf16),
-            vmem((SIDE - 1, BAND, C), bf16),
+            vmem((2, SIDE, SIDE * OWNED, YPART), bf16),
+            vmem((2, SIDE, SIDE * OWNED, C - YPART), bf16),
+            vmem((SIDE, SIDE * OWNED, YPART), bf16),
+            vmem((SIDE, SIDE * OWNED, C - YPART), bf16),
+            vmem((SIDE, SIDE * OWNED, YPART), bf16),
+            vmem((SIDE, SIDE * OWNED, C - YPART), bf16),
+            vmem((SIDE - 1, SIDE * OWNED, YPART), bf16),
+            vmem((SIDE - 1, SIDE * OWNED, C - YPART), bf16),
+            vmem((SIDE, BAND, YPART), bf16),
+            vmem((SIDE, BAND, C - YPART), bf16),
+            vmem((SIDE - 1, BAND, YPART), bf16),
+            vmem((SIDE - 1, BAND, C - YPART), bf16),
             vmem((BAND, C), bf16),
             vmem((SIDE - 1, BAND, C), bf16),
             vmem((ROWS, C), bf16),
             vmem((ROWS, C), bf16),
             vmem((TAPS, OWNED, M), f32),
             vmem((3, C), f32),
-            pltpu.SemaphoreType.DMA((12,)),
+            pltpu.SemaphoreType.DMA((16,)),
             pltpu.SemaphoreType.DMA((COPIES,)),
             pltpu.SemaphoreType.DMA((COPIES,)),
         ],
@@ -519,6 +586,17 @@
             collective_id=0, has_side_effects=True, vmem_limit_bytes=56 * 1024 * 1024
         ),
     )(act, w, ow, cot, don, acc, flag, grad)
+    return pl.pallas_call(
+        store_kernel,
+        name="store_results",
+        out_shape=OUTPUTS,
+        in_specs=[any_space] * 4,
+        out_specs=[any_space] * 4,
+        scratch_shapes=[
+            *(vmem(out.shape, out.dtype) for out in OUTPUTS),
+            pltpu.SemaphoreType.DMA((8,)),
+        ],
+    )(*results)
 
 
 def solution(mesh):

time: 58.7 us -> 46.4 us (0.79)
  local copies, waits for them, and re-layouts: 6.44 us -> 0 us
  Pallas kernels: 51.3 us -> 45.6 us
    unnamed x4 -> x0, local copies, waits for them, and re-layouts: 6.44 us -> none
    pallas_call x1 -> x2, Pallas kernels: 51.3 us -> 45.6 us  [the longest x1 43.6 us: shards(): pl.pallas_call(kernel, name='block_step', out_shape=OUTPUTS, in_specs=[an...]
where the time goes in v2:
time: 46.4 us; the launch traced here: 46.2 us
  Pallas kernels  45.6 us (98%)
  between operations  0.64 us (1%)
    pallas_call x1, Pallas kernels, shards(): pl.pallas_call(kernel, name='block_step', out_shape=OUTPUTS, in_specs=[an...  43.6 us
    pallas_call x1, Pallas kernels, shards(): pl.pallas_call(store_kernel, name='store_results', out_shape=OUTPUTS, in_...  1.98 us

profile of v2, /device:TPU:0, one launch (start us, length us, event | category | flops | bytes accessed | tf_op | source)
XLA Modules:
  0.0 46.2 jit_solution(10360202649843590686)
XLA Ops:
  0.6 43.6 %block_step.1 = (bf16[1,128,1536]{2,1,0:T(8,128)(2,1)}, bf16[1,128,1536]{2,1,0:T(8,128)(2,1)}, f32[5,12,384]{2,1,0:T(8,128)}, f32[3,1536]{1,0:T(4,128)}) custom-call(bf16[1,128,1536]{2,1,0:T(8,128)(2,1)} %act_hbm.1, bf16[5,1536,384]{2,1,0:T(8,128)(2,1)} %w_hbm.1, bf16[384,1536]{1,0:T(8,128)(2,1)} %ow_hbm.1, bf16[1,128,1536]{2,1,0:T(8,128)(2,1)} %cot_hbm.1, ...), custom_call_target="tpu_custom_call" | custom-call | tf_op jit(solution)/shard_map/block_step/pallas_call | solution.py:531
  44.3 2.0 %store_results.1 = (bf16[1,128,1536]{2,1,0:T(8,128)(2,1)}, bf16[1,128,1536]{2,1,0:T(8,128)(2,1)}, f32[5,12,384]{2,1,0:T(8,128)}, f32[3,1536]{1,0:T(4,128)}) custom-call(bf16[1,128,1536]{2,1,0:T(8,128)(2,1)} %get-tuple-element.8.refs_0_, bf16[1,128,1536]{2,1,0:T(8,128)(2,1)} %get-tuple-element.9.refs_1_, f32[5,12,384]{2,1,0:T(8,128)} %get-tuple-element.10.refs_2_, ...), custom_call_target="tpu_custom_call" | custom-call | tf_op jit(solution)/shard_map/store_results/pallas_call | solution.py:589

commit v3 on v2

--- a/solution.py
+++ b/solution.py
@@ -25,10 +25,13 @@
 BAND = 16
 SHARE = DP * OWNED
 YPART = 1024
+PARTS = (slice(0, 128), slice(128, M))
+WIDTHS = tuple(part.stop - part.start for part in PARTS)
+UNITS = ((0, (0, 2), "z"), (0, (1, 3, 4), "y"), (1, (1, 3), "y"), (1, (0, 2, 4), "z"))
+SIZES = tuple((len(taps), WIDTHS[part]) for part, taps, _ in UNITS)
 
 TAP_ORDER = (0, 1, 4, 3, 2)
-NEAR = (1, 7, 2, 6, 3, 5, 4)
-X_EARLY = 7
+FAR = (4, 3, 5, 2, 6, 1, 7)
 
 EPS = 1e-06
 SLOPE = 0.7978845608028654
@@ -109,10 +112,10 @@
     acc_hbm,
     flag_hbm,
     grad_hbm,
-    block_hbm,
-    input_hbm,
-    conv_hbm,
-    out_hbm,
+    block,
+    result,
+    cout,
+    oout,
     act,
     w,
     ow,
@@ -125,8 +128,10 @@
     edge_recv,
     xsend,
     xall,
-    xy_order,
-    xx_order,
+    xedge,
+    xhalo,
+    window_y,
+    window_z,
     gsend,
     grecv,
     hsend,
@@ -134,6 +139,7 @@
     bsend,
     brecv,
     gall,
+    gpad,
     cbuf,
     c1,
     c2,
@@ -152,10 +158,6 @@
     o3_x,
     oz,
     ozr,
-    block,
-    result,
-    cout,
-    oout,
     lsem,
     ssem,
     rsem,
@@ -190,6 +192,15 @@
 
     def y_at(step):
         return lax.rem(y + step, SIDE)
+
+    def x_peer(step):
+        return y * SIDE + x_at(step)
+
+    def y_peer(step):
+        return y_at(step) * SIDE + x
+
+    def z_at(step):
+        return lax.rem(z + step, SIDE)
 
     loads = {}
     for i, (name, src, dst) in enumerate(
@@ -211,38 +222,56 @@
     for step in range(1, SEQ):
         pl.semaphore_signal(barrier, inc=1, device_id={"seq": seq_at(step)}, device_id_type=MESH)
     for step in range(1, SIDE):
+        pl.semaphore_signal(barrier, inc=1, device_id={"dp": y_peer(step)}, device_id_type=MESH)
+        pl.semaphore_signal(barrier, inc=1, device_id={"dp": x_peer(step)}, device_id_type=MESH)
         pl.semaphore_signal(
-            barrier, inc=1, device_id={"dp": y * SIDE + x_at(step)}, device_id_type=MESH
+            barrier, inc=1, device_id={"dp": x_peer(step), "seq": sibling}, device_id_type=MESH
         )
-        pl.semaphore_signal(
-            barrier, inc=1, device_id={"dp": y_at(step) * SIDE + x}, device_id_type=MESH
-        )
-
-    gall[0:EDGE] = jnp.zeros((EDGE, M), bf16)
-    gall[EDGE + LENGTH :] = jnp.zeros((EDGE, M), bf16)
 
     loads["act"].wait()
     act_float = act[...].astype(f32)
     inverse = lax.rsqrt(jnp.mean(act_float * act_float, axis=-1, keepdims=True) + EPS)
     normed = (act_float * inverse).astype(bf16)
 
+    me = x * 2 + core
     column = lax.broadcasted_iota(i32, (1, C), 1)
     owner, lane = column // SHARE, column % SHARE
-    regroup = ones_of(one_hot(C, lane // OWNED * (OWNED * SEQ) + owner * OWNED + lane % OWNED))
-    grouped = dot(normed, regroup)
-    left = lax.broadcasted_iota(i32, (ROWS // 2, 2 * SHARE), 1) < SHARE
-    for pair in range(SEQ // 2):
-        both = grouped[:, pair * 2 * SHARE : (pair + 1) * 2 * SHARE]
-        upper, lower = both[: ROWS // 2], both[ROWS // 2 :]
-        xsend[2 * pair] = jnp.where(left, upper, pltpu.roll(lower, SHARE, 1)).astype(bf16)
-        xsend[2 * pair + 1] = jnp.where(left, pltpu.roll(upper, SHARE, 1), lower).astype(bf16)
-    xall[s] = xsend[s]
-    pl.semaphore_wait(barrier, SEQ - 1 + 2 * (SIDE - 1))
-
-    def send_channels(steps):
-        return [push(xsend.at[seq_at(step)], xall.at[s], seq=seq_at(step)) for step in steps]
-
-    x_copies = send_channels(NEAR[:X_EARLY])
+    device = lane // OWNED
+    channel = (
+        (device // SIDE * SIDE + owner // 2) * (OWNED * SEQ)
+        + (device % SIDE * 2 + owner % 2) * OWNED
+        + lane % OWNED
+    )
+    grouped = dot(normed, ones_of(one_hot(C, channel)))
+    left = lax.broadcasted_iota(i32, (STEP, 2 * SHARE), 1) < SHARE
+    for upper_lower in range(2):
+        for pair in range(SEQ // 2):
+            both = grouped[
+                2 * upper_lower * STEP : 2 * (upper_lower + 1) * STEP, pair * 2 * SHARE : (pair + 1) * 2 * SHARE
+            ]
+            upper, lower = both[:STEP], both[STEP:]
+            xsend[upper_lower, 2 * pair] = jnp.where(left, upper, pltpu.roll(lower, SHARE, 1)).astype(bf16)
+            xsend[upper_lower, 2 * pair + 1] = jnp.where(left, pltpu.roll(upper, SHARE, 1), lower).astype(
+                bf16
+            )
+    xall[me] = xsend[:, me]
+    pl.semaphore_wait(barrier, SEQ - 1 + 3 * (SIDE - 1))
+
+    row_peers = [
+        (step, turn) for step in (2, 1, 3) for turn in range(2)
+    ]
+
+    def row_device(step, turn):
+        seq = sibling if turn else s
+        return x_at(step) * 2 + lax.rem(core + turn, 2), dict(dp=x_peer(step), seq=seq)
+
+    x_copies = []
+    for step, turn in row_peers:
+        to, device_id = row_device(step, turn)
+        x_copies.append(push(xsend.at[:, to], xall.at[me], **device_id))
+    x_copies.append(push(xsend.at[:, x * 2 + 1 - core], xall.at[me], seq=sibling))
+    outer = lax.rem(s + SEQ - 1 + 2 * core, SEQ)
+    edge_rows = push(xsend.at[core], xedge, seq=outer)
 
     taps = {}
     for tap in (0, 1):
@@ -271,7 +300,7 @@
         out[...] = dot(select, rows).astype(bf16)
         own_block(into)[...] = own_block(out)[...]
         copies = []
-        for step in NEAR:
+        for step in FAR:
             peer = seq_at(step)
             src = out.at[pl.ds(pl.multiple_of(peer * PAIR, PAIR), PAIR)]
             copies.append(push(src, own_block(into), seq=peer))
@@ -317,11 +346,14 @@
     hidden = hidden_float.astype(bf16)
     hidden_slots = send_slots(hidden, hsend, hrecv)
 
-    x_copies += send_channels(NEAR[X_EARLY:])
-
-    block[...] = (act[...].astype(f32) + dot(hidden, ow_value)).astype(bf16)
-    block_store = pltpu.make_async_copy(block, block_hbm.at[0], lsem.at[12])
-    block_store.start()
+    edge_rows.wait_recv()
+    xhalo[me] = xedge[me]
+    for step, turn in row_peers:
+        to, device_id = row_device(step, turn)
+        x_copies.append(push(xedge.at[to], xhalo.at[me], **device_id))
+    x_copies.append(push(xedge.at[x * 2 + 1 - core], xhalo.at[me], seq=sibling))
+
+    block[0] = (act[...].astype(f32) + dot(hidden, ow_value)).astype(bf16)
     loads["cot"].wait()
     cot_back = dot_nt(cot[...], ow_value)
     ow_square = dot_nt(ow_value, ow_value).astype(bf16)
@@ -333,14 +365,36 @@
         copy.wait_recv()
     mixed = placed(hrecv).astype(bf16)
     grad_hidden = cot_back + dot(mixed, ow_square)
-    grad_here = pl.ds(pl.multiple_of(EDGE + s * ROWS, EDGE), ROWS)
-    gall[grad_here] = (grad_hidden * slope).astype(bf16)
-
-    def chunk(owner):
-        return gall.at[pl.ds(pl.multiple_of(EDGE + owner * ROWS, EDGE), ROWS)]
-
-    along = [push(chunk(s), chunk(s), seq=seq_at(2 * step)) for step in (1, 3, 2)]
-    across = [push(chunk(s), chunk(s), seq=sibling)]
+    grad_pre = (grad_hidden * slope).astype(bf16)
+    own_rows = pl.ds(pl.multiple_of(me * ROWS, ROWS), ROWS)
+    for part, columns in zip(gall, PARTS):
+        part[own_rows] = grad_pre[:, columns]
+    gpad[EDGE : EDGE + ROWS] = grad_pre
+
+    def chunk(part, owner):
+        return part.at[pl.ds(pl.multiple_of(owner * ROWS, ROWS), ROWS)]
+
+    along, across = [], []
+
+    def spread(part):
+        along.append(
+            [push(chunk(part, me), chunk(part, me), dp=x_peer(step)) for step in (2, 1, 3)]
+        )
+        across.append([push(chunk(part, me), chunk(part, me), seq=sibling)])
+
+    def forward(i):
+        for step, copy in ((1, along[i][1]), (3, along[i][2]), (2, along[i][0])):
+            copy.wait_recv()
+            owner = x_at(SIDE - step) * 2 + core
+            across[i].append(push(chunk(gall[i], owner), chunk(gall[i], owner), seq=sibling))
+
+    spread(gall[0])
+    spread(gall[1])
+    pad_copies = [
+        push(gpad.at[ROWS : ROWS + EDGE], gpad.at[0:EDGE], seq=seq_at(1)),
+        push(gpad.at[EDGE : 2 * EDGE], gpad.at[EDGE + ROWS :], seq=seq_at(SEQ - 1)),
+    ]
+    block_slots = send_slots(block[0], bsend, brecv)
 
     def ordered(first):
         lane = lax.broadcasted_iota(i32, (1, M), 1)
@@ -353,7 +407,7 @@
 
     def out_terms(first, columns):
         hidden_order, mixed_order = ordered(first)
-        terms = dot_tn(hidden_order, cot[:, columns]) + dot_tn(mixed_order, block[:, columns])
+        terms = dot_tn(hidden_order, cot[:, columns]) + dot_tn(mixed_order, block[0, :, columns])
         return terms.astype(bf16).reshape(2, SIDE, SIDE * OWNED, columns.stop - columns.start)
 
     osend_y[...] = out_terms("y", slice(0, YPART))
@@ -372,48 +426,65 @@
         out_first.append(push(obuf_y.at[y_at(step)], o1_y.at[step - 1], dp=y_at(step) * SIDE + x))
         out_first.append(push(obuf_x.at[x_at(step)], o1_x.at[step - 1], dp=y * SIDE + x_at(step)))
 
-    for step, copy in zip((1, 3, 2), along):
-        copy.wait_recv()
-        owner = lax.rem(s + SEQ - 2 * step, SEQ)
-        across.append(push(chunk(owner), chunk(owner), seq=sibling))
-
-    block_slots = send_slots(block[...], bsend, brecv)
-
-    def channels(first):
+    def unpacked(came, first):
         lane = lax.broadcasted_iota(i32, (1, SHARE), 1)
         outer, rest = lane // (SIDE * OWNED), lane % (SIDE * OWNED)
         inner, row = rest // OWNED, rest % OWNED
         device = outer * SIDE + inner if first == "y" else inner * SIDE + outer
+        flat = came.reshape(-1, 2 * SHARE)
         parts = [
-            dot(came, ones_of(one_hot(2 * SHARE, device * OWNED + row + SHARE * lower)))
+            dot(flat, ones_of(one_hot(2 * SHARE, device * OWNED + row + SHARE * lower)))
             for lower in range(2)
         ]
-        parts = [part.astype(bf16).reshape(SEQ, ROWS // 2, SHARE) for part in parts]
-        return jnp.concatenate(parts, axis=1).reshape(LENGTH, SHARE)
+        parts = [part.astype(bf16).reshape(-1, STEP, SHARE) for part in parts]
+        return jnp.concatenate(parts, axis=1)
+
+    def windows(first):
+        middle = unpacked(xall[...], first).reshape(SIDE, 2 * ROWS, SHARE)
+        sides = unpacked(xhalo[...], first).reshape(SIDE, 2, EDGE, SHARE)
+        nothing = jnp.zeros((SIDE, EDGE, SHARE), bf16)
+        return jnp.concatenate(
+            [
+                jnp.where(z > 0, sides[:, 0], nothing),
+                middle,
+                jnp.where(z < SIDE - 1, sides[:, 1], nothing),
+            ],
+            axis=1,
+        )
 
     for copy in x_copies:
         copy.wait_recv()
-    came = xall[...].reshape(SEQ * ROWS // 2, 2 * SHARE)
-    xy_order[...] = channels("y")
-    xx_order[...] = channels("x")
-
-    for copy in across:
-        copy.wait_recv()
-
-    conv_first = []
-    for tap in range(TAPS):
-        start = 2 * EDGE - tap * STEP
-        order = xx_order if tap % 2 == 0 else xy_order
-        term = dot_tn(order[...], gall[start : start + LENGTH])
-        cbuf[tap] = term.astype(bf16).reshape(SIDE, SIDE * OWNED, M)
+    window_y[...] = windows("y")
+    window_z[...] = windows("z")
+
+    def zy_device(axis, step):
+        if axis == "z":
+            return z_at(step), dict(seq=seq_at(2 * step))
+        return y_at(step), dict(dp=y_peer(step))
+
+    def conv_terms(u):
+        part, taps_here, first = UNITS[u]
+        window = window_z if first == "z" else window_y
+        for i, tap in enumerate(taps_here):
+            rows = window[:, tap * STEP : tap * STEP + 2 * ROWS].reshape(LENGTH, SHARE)
+            term = dot_tn(rows, gall[part][...])
+            cbuf[u][i] = term.astype(bf16).reshape(SIDE, SIDE * OWNED, term.shape[1])
         copies = []
-        for step in range(1, SIDE):
-            if tap % 2 == 0:
-                at, peer = x_at(step), y * SIDE + x_at(step)
-            else:
-                at, peer = y_at(step), y_at(step) * SIDE + x
-            copies.append(push(cbuf.at[tap, at], c1.at[tap, step - 1], dp=peer))
-        conv_first.append(copies)
+        for step in (2, 1, 3):
+            at, peer = zy_device(first, step)
+            copies.append(push(cbuf[u].at[:, at], c1[u].at[step - 1], **peer))
+        return copies
+
+    forward(0)
+    for copy in across[0]:
+        copy.wait_recv()
+    conv_first = [conv_terms(0)]
+    forward(1)
+    conv_first.append(conv_terms(1))
+    for copy in across[1]:
+        copy.wait_recv()
+    conv_first.append(conv_terms(2))
+    conv_first.append(conv_terms(3))
 
     band = lax.broadcasted_iota(i32, (SIDE * BAND, SIDE * OWNED), 0)
     packed = lax.broadcasted_iota(i32, (SIDE * BAND, SIDE * OWNED), 1)
@@ -438,30 +509,49 @@
         out_second.append(push(o2_y.at[x_at(step)], o3_y.at[step - 1], dp=y * SIDE + x_at(step)))
         out_second.append(push(o2_x.at[y_at(step)], o3_x.at[step - 1], dp=y_at(step) * SIDE + x))
 
+    for copy in pad_copies:
+        copy.wait_recv()
+
+    @pl.when(s == 0)
+    def _():
+        gpad[0:EDGE] = jnp.zeros((EDGE, M), bf16)
+
+    @pl.when(s == SEQ - 1)
+    def _():
+        gpad[EDGE + ROWS :] = jnp.zeros((EDGE, M), bf16)
+
     grad_normed = jnp.zeros((ROWS, C), f32)
+    for tap in range(TAPS):
+        start = 2 * EDGE - tap * STEP
+        grad_normed = grad_normed + dot_nt(gpad[start : start + ROWS], w[tap])
+
     conv_second = []
-    for tap in range(TAPS):
-        start = pl.multiple_of(s * ROWS + 2 * EDGE - tap * STEP, STEP)
-        grad_normed = grad_normed + dot_nt(gall[pl.ds(start, ROWS)], w[tap])
-        for copy in conv_first[tap]:
+    for u, (part, taps_here, first) in enumerate(UNITS):
+        for copy in conv_first[u]:
             copy.wait_recv()
-        own = cbuf[tap, x] if tap % 2 == 0 else cbuf[tap, y]
-        c2[tap] = banded(summed(own, c1.at[tap]))
+        mine = z if first == "z" else y
+        for i in range(len(taps_here)):
+            total = cbuf[u][i, mine].astype(f32)
+            for step in range(1, SIDE):
+                total = total + c1[u][step - 1, i].astype(f32)
+            c2[u][:, i] = banded(total)
         copies = []
-        for step in range(1, SIDE):
-            if tap % 2 == 0:
-                at, peer = y_at(step), y_at(step) * SIDE + x
-            else:
-                at, peer = x_at(step), y * SIDE + x_at(step)
-            copies.append(push(c2.at[tap, at], c3.at[tap, step - 1], dp=peer))
+        for step in (2, 1, 3):
+            at, peer = zy_device("y" if first == "z" else "z", step)
+            copies.append(push(c2[u].at[at], c3[u].at[step - 1], **peer))
         conv_second.append(copies)
 
     for copy in out_second:
         copy.wait_recv()
-    oz[:, :YPART] = summed(o2_y[x], o3_y).astype(bf16)
-    oz[:, YPART:] = summed(o2_x[y], o3_x).astype(bf16)
+    total = jnp.concatenate([summed(o2_y[x], o3_y), summed(o2_x[y], o3_x)], axis=1)
+    for level in range(SIDE):
+        mine = total[3 * level : 3 * (level + 1)]
+        quarters = [mine[:, i * M : (i + 1) * M] for i in range(SIDE)]
+        oz[level] = jnp.concatenate([*quarters, jnp.zeros((BAND - OWNED, M), f32)], axis=0).astype(
+            bf16
+        )
     out_third = [
-        push(oz, ozr.at[step - 1], seq=seq_at(2 * step)) for step in range(1, SIDE)
+        push(oz.at[z_at(step)], ozr.at[step - 1], seq=seq_at(2 * step)) for step in range(1, SIDE)
     ]
 
     for copy in block_slots:
@@ -469,49 +559,35 @@
     act_float = act[...].astype(f32)
     upstream = (cot[...].astype(f32) + placed(brecv)).astype(bf16)
     spread = jnp.mean(grad_normed * act_float, axis=-1, keepdims=True)
-    result[...] = (
+    result[0] = (
         upstream.astype(f32)
         + inverse * grad_normed
         - inverse * inverse * inverse * act_float * spread
     ).astype(bf16)
-    input_store = pltpu.make_async_copy(result, input_hbm.at[0], lsem.at[13])
-    input_store.start()
-
-    for tap in range(TAPS):
-        for copy in conv_second[tap]:
+    for u, (part, taps_here, first) in enumerate(UNITS):
+        for copy in conv_second[u]:
             copy.wait_recv()
-        total = summed(c2[tap, y] if tap % 2 == 0 else c2[tap, x], c3.at[tap])
-        cout[tap] = total[:OWNED]
-    conv_store = pltpu.make_async_copy(cout, conv_hbm, lsem.at[14])
-    conv_store.start()
+        mine = y if first == "z" else z
+        for i, tap in enumerate(taps_here):
+            total = summed(c2[u][mine, i], c3[u].at[:, i])
+            cout[tap, :, PARTS[part]] = total[:OWNED]
 
     for copy in out_third:
         copy.wait_recv()
-    total = summed(oz[...], ozr)
-    rows = total[0:3]
-    for level in range(1, SIDE):
-        rows = jnp.where(z == level, total[3 * level : 3 * level + 3], rows)
+    total = summed(oz[z], ozr)
+    rows = jnp.concatenate([total[3 * i : 3 * (i + 1)] for i in range(SIDE)], axis=1)
     oout[...] = rows
-    out_store = pltpu.make_async_copy(oout, out_hbm, lsem.at[15])
-    out_store.start()
-
     for copy in pending:
         copy.wait_send()
-    for store in (block_store, input_store, conv_store, out_store):
-        store.wait()
-
-
-COPIES = 2 + 7 + 7 + 7 + 7 + 3 + 4 + 2 + 6 + 15 + 6 + 15 + 3
+
+
+COPIES = 2 + 7 + 8 + 7 + 7 + 7 + 2 * (3 + 4) + 2 + 2 + 6 + 12 + 6 + 12 + 3
 
 
 def store_kernel(*refs):
-    came, left, held, sem = refs[:4], refs[4:8], refs[8:12], refs[12]
-    loads = [pltpu.make_async_copy(came[i], held[i], sem.at[i]) for i in range(4)]
-    stores = [pltpu.make_async_copy(held[i], left[i], sem.at[4 + i]) for i in range(4)]
-    for load in loads:
-        load.start()
-    for load, store in zip(loads, stores):
-        load.wait()
+    came, left, sem = refs[:4], refs[4:8], refs[8]
+    stores = [pltpu.make_async_copy(came[i], left[i], sem.at[i]) for i in range(4)]
+    for store in stores:
         store.start()
     for store in stores:
         store.wait()
@@ -531,9 +607,9 @@
     results = pl.pallas_call(
         kernel,
         name="block_step",
-        out_shape=OUTPUTS,
-        in_specs=[any_space] * 8,
-        out_specs=[any_space] * 4,
+        out_shape=tuple(vmem(o.shape, o.dtype) for o in OUTPUTS),
+        in_specs=[pl.BlockSpec(memory_space=pltpu.HBM)] * 8,
+        out_specs=[pl.BlockSpec(memory_space=vmem)] * 4,
         scratch_shapes=[
             vmem((ROWS, C), bf16),
             vmem((TAPS, C, M), bf16),
@@ -545,21 +621,24 @@
             vmem((1, JUNC), f32),
             vmem((2, EDGE, M), bf16),
             vmem((2, EDGE, M), bf16),
-            vmem((SEQ, ROWS // 2, 2 * SHARE), bf16),
-            vmem((SEQ, ROWS // 2, 2 * SHARE), bf16),
-            vmem((LENGTH, SHARE), bf16),
-            vmem((LENGTH, SHARE), bf16),
+            vmem((2, SEQ, STEP, 2 * SHARE), bf16),
+            vmem((SEQ, 2, STEP, 2 * SHARE), bf16),
+            vmem((SEQ, STEP, 2 * SHARE), bf16),
+            vmem((SEQ, STEP, 2 * SHARE), bf16),
+            vmem((SIDE, 2 * (ROWS + EDGE), SHARE), bf16),
+            vmem((SIDE, 2 * (ROWS + EDGE), SHARE), bf16),
             vmem((SLOTS, M), bf16),
             vmem((SLOTS, M), bf16),
             vmem((SLOTS, M), bf16),
             vmem((SLOTS, M), bf16),
             vmem((SLOTS, C), bf16),
             vmem((SLOTS, C), bf16),
-            vmem((LENGTH + 2 * EDGE, M), bf16),
-            vmem((TAPS, SIDE, SIDE * OWNED, M), bf16),
-            vmem((TAPS, SIDE - 1, SIDE * OWNED, M), bf16),
-            vmem((TAPS, SIDE, BAND, M), bf16),
-            vmem((TAPS, SIDE - 1, BAND, M), bf16),
+            [vmem((LENGTH, width), bf16) for width in WIDTHS],
+            vmem((ROWS + 2 * EDGE, M), bf16),
+            [vmem((n, SIDE, SIDE * OWNED, width), bf16) for n, width in SIZES],
+            [vmem((SIDE - 1, n, SIDE * OWNED, width), bf16) for n, width in SIZES],
+            [vmem((SIDE, n, BAND, width), bf16) for n, width in SIZES],
+            [vmem((SIDE - 1, n, BAND, width), bf16) for n, width in SIZES],
             vmem((2, SIDE, SIDE * OWNED, YPART), bf16),
             vmem((2, SIDE, SIDE * OWNED, C - YPART), bf16),
             vmem((SIDE, SIDE * OWNED, YPART), bf16),
@@ -572,13 +651,9 @@
             vmem((SIDE, BAND, C - YPART), bf16),
             vmem((SIDE - 1, BAND, YPART), bf16),
             vmem((SIDE - 1, BAND, C - YPART), bf16),
-            vmem((BAND, C), bf16),
-            vmem((SIDE - 1, BAND, C), bf16),
-            vmem((ROWS, C), bf16),
-            vmem((ROWS, C), bf16),
-            vmem((TAPS, OWNED, M), f32),
-            vmem((3, C), f32),
-            pltpu.SemaphoreType.DMA((16,)),
+            vmem((SIDE, BAND, M), bf16),
+            vmem((SIDE - 1, BAND, M), bf16),
+            pltpu.SemaphoreType.DMA((12,)),
             pltpu.SemaphoreType.DMA((COPIES,)),
             pltpu.SemaphoreType.DMA((COPIES,)),
         ],
@@ -590,13 +665,10 @@
         store_kernel,
         name="store_results",
         out_shape=OUTPUTS,
-        in_specs=[any_space] * 4,
+        in_specs=[pl.BlockSpec(memory_space=vmem)] * 4,
         out_specs=[any_space] * 4,
-        scratch_shapes=[
-            *(vmem(out.shape, out.dtype) for out in OUTPUTS),
-            pltpu.SemaphoreType.DMA((8,)),
-        ],
-    )(*results)
+        scratch_shapes=[pltpu.SemaphoreType.DMA((4,))],
+    )(*(pltpu.with_memory_space_constraint(r, pltpu.VMEM) for r in results))
 
 
 def solution(mesh):

time: 46.4 us -> 40.6 us (0.88)
  Pallas kernels: 45.6 us -> 39.7 us
    pallas_call x1, Pallas kernels: 43.6 us -> 38.7 us  [shards(): pl.pallas_call(kernel, name='block_step', out_shape=tuple((vmem(o.shape,...]
    pallas_call x1, Pallas kernels: 1.98 us -> 0.95 us  [shards(): pl.pallas_call(store_kernel, name='store_results', out_shape=OUTPUTS, in_...]
where the time goes in v3:
time: 40.6 us; the launch traced here: 40.5 us
  Pallas kernels  39.7 us (98%)
  between operations  0.8 us (2%)
    pallas_call x1, Pallas kernels, shards(): pl.pallas_call(kernel, name='block_step', out_shape=tuple((vmem(o.shape,...  38.7 us
    pallas_call x1, Pallas kernels, shards(): pl.pallas_call(store_kernel, name='store_results', out_shape=OUTPUTS, in_...  0.95 us

profile of v3, /device:TPU:0, one launch (start us, length us, event | category | flops | bytes accessed | tf_op | source)
XLA Modules:
  0.0 40.5 jit_solution(10179872723737685235)
XLA Ops:
  0.6 38.7 %block_step.1 = (bf16[1,128,1536]{2,1,0:T(8,128)(2,1)S(1)}, bf16[1,128,1536]{2,1,0:T(8,128)(2,1)S(1)}, f32[5,12,384]{2,1,0:T(8,128)S(1)}, f32[3,1536]{1,0:T(4,128)S(1)}) custom-call(bf16[1,128,1536]{2,1,0:T(8,128)(2,1)} %act_hbm.1, bf16[5,1536,384]{2,1,0:T(8,128)(2,1)} %w_hbm.1, bf16[384,1536]{1,0:T(8,128)(2,1)} %ow_hbm.1, bf16[1,128,1536]{2,1,0:T(8,128)(2,1)} %cot_hbm.1, ...), custom_call_target="tpu_custom_call" | custom-call | tf_op jit(solution)/shard_map/block_step/pallas_call | solution.py:607
  39.4 0.9 %store_results.1 = (bf16[1,128,1536]{2,1,0:T(8,128)(2,1)}, bf16[1,128,1536]{2,1,0:T(8,128)(2,1)}, f32[5,12,384]{2,1,0:T(8,128)}, f32[3,1536]{1,0:T(4,128)}) custom-call(bf16[1,128,1536]{2,1,0:T(8,128)(2,1)S(1)} %get-tuple-element.8.refs_0_, bf16[1,128,1536]{2,1,0:T(8,128)(2,1)S(1)} %get-tuple-element.9.refs_1_, f32[5,12,384]{2,1,0:T(8,128)S(1)} %get-tuple-element.10.refs_2_, ...), custom_call_target="tpu_custom_call" | custom-call | tf_op jit(solution)/shard_map/store_results/pallas_call | solution.py:664

commit v4 on v3

--- a/solution.py
+++ b/solution.py
@@ -27,7 +27,7 @@
 YPART = 1024
 PARTS = (slice(0, 128), slice(128, M))
 WIDTHS = tuple(part.stop - part.start for part in PARTS)
-UNITS = ((0, (0, 2), "z"), (0, (1, 3, 4), "y"), (1, (1, 3), "y"), (1, (0, 2, 4), "z"))
+UNITS = ((0, (0, 2), "z"), (0, (1, 3, 4), "y"), (1, (0, 2, 4), "z"), (1, (1, 3), "y"))
 SIZES = tuple((len(taps), WIDTHS[part]) for part, taps, _ in UNITS)
 
 TAP_ORDER = (0, 1, 4, 3, 2)
@@ -100,7 +100,7 @@
         at_don = jnp.where(don_at, wide, 0.0).astype(bf16)
         return (dot_nt(at_acc, came_don) + dot_nt(at_don, came_acc)).astype(bf16)
 
-    return select, placing(high), placing(low)
+    return select, jnp.concatenate([placing(high), placing(low)], axis=0)
 
 
 def kernel(
@@ -265,14 +265,14 @@
         seq = sibling if turn else s
         return x_at(step) * 2 + lax.rem(core + turn, 2), dict(dp=x_peer(step), seq=seq)
 
+    outer = lax.rem(s + SEQ - 1 + 2 * core, SEQ)
+    edge_rows = push(xsend.at[core], xedge, seq=outer)
+
     x_copies = []
     for step, turn in row_peers:
         to, device_id = row_device(step, turn)
         x_copies.append(push(xsend.at[:, to], xall.at[me], **device_id))
     x_copies.append(push(xsend.at[:, x * 2 + 1 - core], xall.at[me], seq=sibling))
-    outer = lax.rem(s + SEQ - 1 + 2 * core, SEQ)
-    edge_rows = push(xsend.at[core], xedge, seq=outer)
-
     taps = {}
     for tap in (0, 1):
         loads[f"w{tap}"].wait()
@@ -291,7 +291,7 @@
     behind = push(edge_send.at[1], edge_recv.at[1], seq=seq_at(SEQ - 1))
     for name in ("don", "acc", "flag", "grad"):
         loads[name].wait()
-    select, place_high, place_low = junction_matrices(s, don[...], acc[...], flag[...], grad[...])
+    select, place_both = junction_matrices(s, don[...], acc[...], flag[...], grad[...])
 
     def own_block(ref):
         return ref.at[pl.ds(pl.multiple_of(s * PAIR, PAIR), PAIR)]
@@ -307,12 +307,20 @@
         return copies
 
     def placed(ref):
-        return dot(place_high, ref[...]) + dot(place_low, ref[...])
+        both = dot(place_both, ref[...])
+        return both[:ROWS] + both[ROWS:]
 
     loads["ow"].wait()
     ow_value = ow[...]
     act_back = dot_nt(act[...], ow_value).astype(bf16)
     act_slots = send_slots(act_back, gsend, grecv)
+
+    edge_rows.wait_recv()
+    xhalo[me] = xedge[me]
+    for step, turn in row_peers:
+        to, device_id = row_device(step, turn)
+        x_copies.append(push(xedge.at[to], xhalo.at[me], **device_id))
+    x_copies.append(push(xedge.at[x * 2 + 1 - core], xhalo.at[me], seq=sibling))
 
     loads["w2"].wait()
     preact = dot(normed, w[2])
@@ -346,17 +354,11 @@
     hidden = hidden_float.astype(bf16)
     hidden_slots = send_slots(hidden, hsend, hrecv)
 
-    edge_rows.wait_recv()
-    xhalo[me] = xedge[me]
-    for step, turn in row_peers:
-        to, device_id = row_device(step, turn)
-        x_copies.append(push(xedge.at[to], xhalo.at[me], **device_id))
-    x_copies.append(push(xedge.at[x * 2 + 1 - core], xhalo.at[me], seq=sibling))
-
     block[0] = (act[...].astype(f32) + dot(hidden, ow_value)).astype(bf16)
     loads["cot"].wait()
-    cot_back = dot_nt(cot[...], ow_value)
-    ow_square = dot_nt(ow_value, ow_value).astype(bf16)
+    backs = dot_nt(jnp.concatenate([cot[...], ow_value], axis=0), ow_value)
+    cot_back = backs[:ROWS]
+    ow_square = backs[ROWS:].astype(bf16)
 
     for copy in act_slots:
         copy.wait_recv()
@@ -403,11 +405,11 @@
         inner, rest = rest // OWNED, rest % OWNED
         device = outer * SIDE + inner if first == "y" else inner * SIDE + outer
         order = ones_of(one_hot(M, device * 3 * SEQ + rest // 3 * 6 + half * 3 + rest % 3))
-        return dot(hidden, order).astype(bf16), dot(mixed, order).astype(bf16)
+        return dot(jnp.concatenate([hidden, mixed], axis=0), order).astype(bf16)
 
     def out_terms(first, columns):
-        hidden_order, mixed_order = ordered(first)
-        terms = dot_tn(hidden_order, cot[:, columns]) + dot_tn(mixed_order, block[0, :, columns])
+        rows = jnp.concatenate([cot[:, columns], block[0, :, columns]], axis=0)
+        terms = dot_tn(ordered(first), rows)
         return terms.astype(bf16).reshape(2, SIDE, SIDE * OWNED, columns.stop - columns.start)
 
     osend_y[...] = out_terms("y", slice(0, YPART))

time: 40.6 us -> 40.1 us (0.988)
  no operation moved by 1% of the time
where the time goes in v4:
time: 40.1 us; the launch traced here: 40 us
  Pallas kernels  39.3 us (98%)
  between operations  0.64 us (2%)
    pallas_call x1, Pallas kernels, shards(): pl.pallas_call(kernel, name='block_step', out_shape=tuple((vmem(o.shape,...  38.4 us
    pallas_call x1, Pallas kernels, shards(): pl.pallas_call(store_kernel, name='store_results', out_shape=OUTPUTS, in_...  0.95 us

profile of v4, /device:TPU:0, one launch (start us, length us, event | category | flops | bytes accessed | tf_op | source)
XLA Modules:
  0.0 40.0 jit_solution(5712157558826359822)
XLA Ops:
  0.6 38.4 %block_step.1 = (bf16[1,128,1536]{2,1,0:T(8,128)(2,1)S(1)}, bf16[1,128,1536]{2,1,0:T(8,128)(2,1)S(1)}, f32[5,12,384]{2,1,0:T(8,128)S(1)}, f32[3,1536]{1,0:T(4,128)S(1)}) custom-call(bf16[1,128,1536]{2,1,0:T(8,128)(2,1)} %act_hbm.1, bf16[5,1536,384]{2,1,0:T(8,128)(2,1)} %w_hbm.1, bf16[384,1536]{1,0:T(8,128)(2,1)} %ow_hbm.1, bf16[1,128,1536]{2,1,0:T(8,128)(2,1)} %cot_hbm.1, ...), custom_call_target="tpu_custom_call" | custom-call | tf_op jit(solution)/shard_map/block_step/pallas_call | solution.py:609
  39.0 0.9 %store_results.1 = (bf16[1,128,1536]{2,1,0:T(8,128)(2,1)}, bf16[1,128,1536]{2,1,0:T(8,128)(2,1)}, f32[5,12,384]{2,1,0:T(8,128)}, f32[3,1536]{1,0:T(4,128)}) custom-call(bf16[1,128,1536]{2,1,0:T(8,128)(2,1)S(1)} %get-tuple-element.8.refs_0_, bf16[1,128,1536]{2,1,0:T(8,128)(2,1)S(1)} %get-tuple-element.9.refs_1_, f32[5,12,384]{2,1,0:T(8,128)S(1)} %get-tuple-element.10.refs_2_, ...), custom_call_target="tpu_custom_call" | custom-call | tf_op jit(solution)/shard_map/store_results/pallas_call | solution.py:666

commit v5 on v4

--- a/solution.py
+++ b/solution.py
@@ -216,7 +216,8 @@
         )
     ):
         loads[name] = pltpu.make_async_copy(src, dst, lsem.at[i])
-        loads[name].start()
+        if name == "act":
+            loads[name].start()
 
     barrier = pltpu.get_barrier_semaphore()
     for step in range(1, SEQ):
@@ -227,6 +228,9 @@
         pl.semaphore_signal(
             barrier, inc=1, device_id={"dp": x_peer(step), "seq": sibling}, device_id_type=MESH
         )
+
+    for name in list(loads)[1:]:
+        loads[name].start()
 
     loads["act"].wait()
     act_float = act[...].astype(f32)
@@ -588,7 +592,12 @@
 
 def store_kernel(*refs):
     came, left, sem = refs[:4], refs[4:8], refs[8]
-    stores = [pltpu.make_async_copy(came[i], left[i], sem.at[i]) for i in range(4)]
+    pieces = [
+        (came[i].at[:, rows], left[i].at[:, rows])
+        for rows in (pl.ds(start, STEP) for start in range(0, ROWS, STEP))
+        for i in range(2)
+    ] + [(came[i], left[i]) for i in range(2, 4)]
+    stores = [pltpu.make_async_copy(*piece, sem.at[i]) for i, piece in enumerate(pieces)]
     for store in stores:
         store.start()
     for store in stores:
@@ -669,7 +678,7 @@
         out_shape=OUTPUTS,
         in_specs=[pl.BlockSpec(memory_space=vmem)] * 4,
         out_specs=[any_space] * 4,
-        scratch_shapes=[pltpu.SemaphoreType.DMA((4,))],
+        scratch_shapes=[pltpu.SemaphoreType.DMA((2 * (ROWS // STEP) + 2,))],
     )(*(pltpu.with_memory_space_constraint(r, pltpu.VMEM) for r in results))
 
 

time: 40.1 us -> 40.3 us (level)
  no operation moved by 1% of the time
where the time goes in v5:
time: 40.3 us; the launch traced here: 40.2 us
  Pallas kernels  39.4 us (98%)
  between operations  0.8 us (2%)
    pallas_call x1, Pallas kernels, shards(): pl.pallas_call(kernel, name='block_step', out_shape=tuple((vmem(o.shape,...  38.4 us
    pallas_call x1, Pallas kernels, shards(): pl.pallas_call(store_kernel, name='store_results', out_shape=OUTPUTS, in_...  1 us

profile of v5, /device:TPU:0, one launch (start us, length us, event | category | flops | bytes accessed | tf_op | source)
XLA Modules:
  0.0 40.2 jit_solution(15759433724887781722)
XLA Ops:
  0.6 38.4 %block_step.1 = (bf16[1,128,1536]{2,1,0:T(8,128)(2,1)S(1)}, bf16[1,128,1536]{2,1,0:T(8,128)(2,1)S(1)}, f32[5,12,384]{2,1,0:T(8,128)S(1)}, f32[3,1536]{1,0:T(4,128)S(1)}) custom-call(bf16[1,128,1536]{2,1,0:T(8,128)(2,1)} %act_hbm.1, bf16[5,1536,384]{2,1,0:T(8,128)(2,1)} %w_hbm.1, bf16[384,1536]{1,0:T(8,128)(2,1)} %ow_hbm.1, bf16[1,128,1536]{2,1,0:T(8,128)(2,1)} %cot_hbm.1, ...), custom_call_target="tpu_custom_call" | custom-call | tf_op jit(solution)/shard_map/block_step/pallas_call | solution.py:618
  39.0 1.0 %store_results.1 = (bf16[1,128,1536]{2,1,0:T(8,128)(2,1)}, bf16[1,128,1536]{2,1,0:T(8,128)(2,1)}, f32[5,12,384]{2,1,0:T(8,128)}, f32[3,1536]{1,0:T(4,128)}) custom-call(bf16[1,128,1536]{2,1,0:T(8,128)(2,1)S(1)} %get-tuple-element.8.refs_0_, bf16[1,128,1536]{2,1,0:T(8,128)(2,1)S(1)} %get-tuple-element.9.refs_1_, f32[5,12,384]{2,1,0:T(8,128)S(1)} %get-tuple-element.10.refs_2_, ...), custom_call_target="tpu_custom_call" | custom-call | tf_op jit(solution)/shard_map/store_results/pallas_call | solution.py:675
